TPU v7x, 32 devices: a whole 2x2x4 slice. The times are simulated.
32 devices in a mesh: dp: 4 (over y, x), node: 4 (over z), dev: 2 (over core).
Axes of the slice: x: 2, y: 2, z: 4, core: 2. Of those that a mesh axis runs over, the one named last changes fastest.
Arguments:
- tokens: bfloat16 [4096, 3584], P(('dp', 'node', 'dev')), may hold values from -6 to 6
- cotangent: bfloat16 [4096, 3584], P(('dp', 'node', 'dev')), may hold values from -6 to 6
- routes: int32 [4096, 1], P(('dp', 'node', 'dev')), may hold values from 0 to 3; in each aligned block of 128 rows (0 to 127, 128 to 255, ...) at most 36 rows name the same one
- gates: float32 [4096, 1], P(('dp', 'node', 'dev')), may hold values from 0.05 to 1
- w_gate: bfloat16 [4, 3584, 1024], P('node', None, 'dev'), may hold values from -0.09375 to 0.09375
- w_up: bfloat16 [4, 3584, 1024], P('node', None, 'dev'), may hold values from -0.09375 to 0.09375
- w_down: bfloat16 [4, 1024, 3584], P('node', 'dev'), may hold values from -0.1875 to 0.1875
Outputs:
- mixed_out: bfloat16 [4096, 3584], P(('dp', 'node', 'dev'))
- grad_down: bfloat16 [4, 1024, 3584], P('node', 'dev')
Inputs may be any that keep to these rules, and one draw needn't show every extreme that they name: `routes`: each token names 1 different experts; among the 128 tokens of one device at most 36 name any one expert, and in every draw some device has an expert named by exactly 36 of its tokens.
All inputs are finite; a program needn't handle non-finite values.
Results may differ from a plain program's by a relative error of at most 0.009.
Values may be sent and summed in bfloat16 or wider, within the bound.
No kernel may reach another device: no remote copies, remote signals or barrier semaphores. Data moves between devices by JAX's collectives and lax.ppermute only.
A program may use at most 64 MiB of HBM per device.

v0:
```python
import jax
import jax.numpy as jnp
from jax import lax
from jax.sharding import PartitionSpec as P


def expert_rows(inputs_in, grads_in, w_gate, w_up, w_down):
    all_inputs, all_grads = (
        lax.all_gather(inputs_in, "dev", axis=0, tiled=True),
        lax.all_gather(grads_in, "dev", axis=0, tiled=True),
    )
    gate_proj = jnp.einsum("scd,df->scf", all_inputs, w_gate[0], preferred_element_type=jnp.float32)
    up_proj = jnp.einsum("scd,df->scf", all_inputs, w_up[0], preferred_element_type=jnp.float32)
    hidden = (jax.nn.silu(gate_proj) * up_proj).astype(jnp.bfloat16)
    partial_value = jnp.einsum("scf,fd->scd", hidden, w_down[0], preferred_element_type=jnp.float32)
    summed = lax.psum_scatter(
        partial_value.astype(jnp.bfloat16), "dev", scatter_dimension=0, tiled=True
    )
    return (summed, hidden, all_grads)


def send_back(expert_out):
    return lax.all_to_all(expert_out, "node", split_axis=0, concat_axis=0, tiled=True)


def per_device(tokens, cotangent, routes, gates, w_gate, w_up, w_down):
    tok_count = tokens.shape[0]
    top_count = routes.shape[1]
    experts = w_gate.shape[0] * lax.axis_size("node")
    capacity = (tok_count * top_count * 9 + 8 * experts - 1) // (8 * experts)
    flat_routes = routes.reshape(-1)
    hits = (flat_routes[:, None] == jnp.arange(experts, dtype=jnp.int32)[None, :]).astype(jnp.int32)
    before = jnp.cumsum(hits, axis=0) - hits
    target = flat_routes * capacity + jnp.sum(before * hits, axis=1)
    placer = (target[:, None] == jnp.arange(experts * capacity, dtype=jnp.int32)[None, :]).astype(
        jnp.bfloat16
    )
    token_rows = jnp.repeat(tokens, top_count, axis=0)
    weighted = (
        gates.reshape(-1)[:, None] * jnp.repeat(cotangent, top_count, axis=0).astype(jnp.float32)
    ).astype(jnp.bfloat16)
    input_buffer = (
        jnp.einsum("rs,rd->sd", placer, token_rows, preferred_element_type=jnp.float32)
        .astype(jnp.bfloat16)
        .reshape(experts, capacity, -1)
    )
    grad_buffer = (
        jnp.einsum("rs,rd->sd", placer, weighted, preferred_element_type=jnp.float32)
        .astype(jnp.bfloat16)
        .reshape(experts, capacity, -1)
    )
    inputs_in, grads_in = (
        lax.all_to_all(input_buffer, "node", split_axis=0, concat_axis=0, tiled=True),
        lax.all_to_all(grad_buffer, "node", split_axis=0, concat_axis=0, tiled=True),
    )
    summed, hidden, all_grads = expert_rows(inputs_in, grads_in, w_gate, w_up, w_down)
    returned_rows = send_back(summed)
    grad_part = jnp.einsum("scf,scd->fd", hidden, all_grads, preferred_element_type=jnp.float32)
    grad_total = lax.psum(grad_part.astype(jnp.bfloat16), "dp")
    expert_out = jnp.dot(
        placer, returned_rows.reshape(experts * capacity, -1), preferred_element_type=jnp.float32
    )
    mixed_out = jnp.sum(gates[:, :, None] * expert_out.reshape(tok_count, top_count, -1), axis=1)
    return (mixed_out.astype(jnp.bfloat16), grad_total[None])


def solution(mesh):
    placed = (
        P(("dp", "node", "dev"), None),
        P(("dp", "node", "dev"), None),
        P(("dp", "node", "dev"), None),
        P(("dp", "node", "dev"), None),
        P("node", None, "dev"),
        P("node", None, "dev"),
        P("node", "dev", None),
    )
    return jax.shard_map(
        per_device,
        mesh=mesh,
        in_specs=placed,
        out_specs=(P(("dp", "node", "dev"), None), P("node", "dev", None)),
        check_vma=False,
    )
```

profile of v0, /device:TPU:0, one launch (start us, length us, event | category | flops | bytes accessed | tf_op | source)
XLA Modules:
  0.0 212.0 jit_solution(3575032232446568098)
XLA Ops:
  7.2 0.0 copy-start
  7.2 0.0 all-gather.3.cloned.1.call-start
  7.2 0.8 fusion.17
  8.0 0.2 reduce_window_sum.11
  8.2 0.8 select_reduce_fusion
  9.0 0.7 fusion.18
  9.7 0.0 copy-done
  9.7 0.5 convolution_convert_fusion.2
  10.3 0.0 copy-start.1
  10.3 0.3 reshape.22
  10.5 34.1 %all_to_all.15 = bf16[4,36,3584]{2,1,0:T(8,128)(2,1)} all-to-all(bf16[4,36,3584]{2,1,0:T(8,128)(2,1)S(1)} %reshape.22), channel_id=1, replica_groups=mesh['dp'=4,'node'=4,'dev'=2] {'node'}, dimensions={0} | all-to-all | bytes 2064384 | tf_op jit(solution)/shard_map/all_to_all | solution.py:53
  44.6 0.0 all-gather.3.cloned.1.call-update
  44.6 0.0 all-gather.5.cloned.1.call-start
  44.7 0.0 copy-done.1
  44.7 1.7 convolution_convert_fusion.1
  46.4 0.3 reshape.24
  46.7 30.2 %all_to_all.16 = bf16[4,36,3584]{2,1,0:T(8,128)(2,1)} all-to-all(bf16[4,36,3584]{2,1,0:T(8,128)(2,1)S(1)} %reshape.24), channel_id=1, replica_groups=mesh['dp'=4,'node'=4,'dev'=2] {'node'}, dimensions={0} | all-to-all | bytes 2064384 | tf_op jit(solution)/shard_map/all_to_all | solution.py:54
  76.9 0.0 all-gather.5.cloned.1.call-update
  76.9 0.0 reduce-scatter.2.cloned.1.call-start
  77.0 0.0 all-gather.3.cloned.1.call-done
  77.0 0.0 copy-start.2
  77.0 0.0 copy-start.4
  77.0 4.2 %fusion.5 = f32[8,36,512]{2,1,0:T(8,128)S(1)} fusion(bf16[8,36,3584]{2,1,0:T(8,128)(2,1)} %all-gather.3.cloned.1.call-done, bf16[1,3584,512]{2,1,0:T(8,128)(2,1)} %param.11), kind=kOutput, calls=%fused_computation.10 | convolution fusion | flops 1056964608 | bytes 6324224 | tf_op jit(solution)/shard_map/scd,df->scf/dot_general | solution.py:12
  81.3 0.0 copy-done.2
  81.3 0.2 copy-done.4
  81.5 0.0 copy-start.3
  81.5 1.4 fusion.10
  83.0 0.9 copy-done.3
  83.9 2.8 %convolution_convert_fusion = bf16[8,36,3584]{2,1,0:T(8,128)(2,1)} fusion(bf16[8,36,512]{2,1,0:T(8,128)(2,1)S(1)} %fusion.10, bf16[1,512,3584]{2,1,0:T(8,128)(2,1)S(1)} %copy-done.3), kind=kOutput, calls=%fused_computation.2 | convolution fusion | flops 1057996800 | bytes 6029312 | tf_op jit(solution)/shard_map/scf,fd->scd/dot_general | solution.py:15
  86.7 0.0 reduce-scatter.2.cloned.1.call-update
  86.7 0.0 all-reduce.2.cloned.1.call-start
  86.8 0.3 all-gather.5.cloned.1.call-done
  87.1 5.6 %fusion = bf16[1,512,3584]{2,1,0:T(8,128)(2,1)} fusion(bf16[8,36,512]{2,1,0:T(8,128)(2,1)S(1)} %fusion.10, bf16[8,36,3584]{2,1,0:T(8,128)(2,1)} %all-gather.5.cloned.1.call-done), kind=kOutput, calls=%fused_computation.1 | convolution fusion | flops 1058799616 | bytes 6029312 | tf_op jit(solution)/shard_map/scf,scd->fd/dot_general | solution.py:58
  92.7 0.0 all-reduce.2.cloned.1.call-update
  92.7 7.7 %reduce-scatter.2.cloned.1.call-done = bf16[4,36,3584]{2,1,0:T(8,128)(2,1)} async-done(((bf16[8,36,3584]{2,1,0:T(8,128)(2,1)}), bf16[4,36,3584]{2,1,0:T(8,128)(2,1)}) %reduce-scatter.2.cloned.1.call-update) | async-done | bytes 1032208 | tf_op jit(solution)/shard_map/reduce_scatter | solution.py:16
  100.4 33.2 %all_to_all.17 = bf16[4,36,3584]{2,1,0:T(8,128)(2,1)S(1)} all-to-all(bf16[4,36,3584]{2,1,0:T(8,128)(2,1)} %reduce-scatter.2.cloned.1.call-done), channel_id=1, replica_groups=mesh['dp'=4,'node'=4,'dev'=2] {'node'}, dimensions={0} | all-to-all | bytes 2064384 | tf_op jit(solution)/shard_map/all_to_all | solution.py:23
  133.5 0.2 reshape.23
  133.8 1.4 fusion.1
  135.2 66.2 %all-reduce.2.cloned.1.call-done = bf16[1,512,3584]{2,1,0:T(8,128)(2,1)} async-done(((bf16[1,512,3584]{2,1,0:T(8,128)(2,1)}), bf16[1,512,3584]{2,1,0:T(8,128)(2,1)}) %all-reduce.2.cloned.1.call-update) | async-done | bytes 3670032 | tf_op jit(solution)/shard_map/psum | solution.py:59
  201.4 4.1 %copy.10 = bf16[1,512,3584]{2,1,0:T(8,128)(2,1)} copy(bf16[1,512,3584]{2,1,0:T(8,128)(2,1)} %all-reduce.2.cloned.1.call-done) | data formatting | bytes 7340032
Async XLA Ops:
  7.2 2.6 %copy-start = (bf16[128,3584]{1,0:T(8,128)(2,1)S(1)}, bf16[128,3584]{1,0:T(8,128)(2,1)}, u32[]{:S(2)}) copy-start(bf16[128,3584]{1,0:T(8,128)(2,1)} %param.7) | copy-start | bytes 2752516
  7.2 69.8 %all-gather.3.cloned.1.call-start = ((), (), s32[]{:S(2)}) async-start(), calls=%async_computation.4 | async-start | bytes 3440640 | tf_op jit(solution)/shard_map/all_gather | solution.py:9
  10.3 34.4 %copy-start.1 = (f32[128,1]{0,1:T(1,128)S(1)}, f32[128,1]{0,1:T(1,128)}, u32[]{:S(2)}) copy-start(f32[128,1]{0,1:T(1,128)} %param.10) | copy-start | bytes 1540
  44.6 42.5 %all-gather.5.cloned.1.call-start = ((), (), s32[]{:S(2)}) async-start(), calls=%async_computation.6 | async-start | bytes 3440640 | tf_op jit(solution)/shard_map/all_gather | solution.py:10
  76.9 23.5 %reduce-scatter.2.cloned.1.call-start = ((), (), s32[]{:S(2)}) async-start(), calls=%async_computation.5 | async-start | bytes 3440640 | tf_op jit(solution)/shard_map/reduce_scatter | solution.py:16
  77.0 4.3 %copy-start.2 = (bf16[1,3584,512]{2,1,0:T(8,128)(2,1)S(1)}, bf16[1,3584,512]{2,1,0:T(8,128)(2,1)}, u32[]{:S(2)}) copy-start(bf16[1,3584,512]{2,1,0:T(8,128)(2,1)} %param.12) | copy-start | bytes 11010052
  77.0 4.5 %copy-start.4 = (bf16[8,36,3584]{2,1,0:T(8,128)(2,1)S(1)}, bf16[8,36,3584]{2,1,0:T(8,128)(2,1)}, u32[]{:S(2)}) copy-start(bf16[8,36,3584]{2,1,0:T(8,128)(2,1)} %all-gather.3.cloned.1.call-done) | copy-start | bytes 6193156
  81.5 2.4 %copy-start.3 = (bf16[1,512,3584]{2,1,0:T(8,128)(2,1)S(1)}, bf16[1,512,3584]{2,1,0:T(8,128)(2,1)}, u32[]{:S(2)}) copy-start(bf16[1,512,3584]{2,1,0:T(8,128)(2,1)} %param.13) | copy-start | bytes 11010052
  86.7 114.7 %all-reduce.2.cloned.1.call-start = ((), (), s32[]{:S(2)}) async-start(), calls=%async_computation.7 | async-start | bytes 7340032 | tf_op jit(solution)/shard_map/psum | solution.py:59
Sparse Core Ops, SparseCore 0:
  44.7 9.9 all-gather.2
  77.0 9.9 all-gather.4
  89.4 10.9 reduce-scatter.1
  104.2 97.1 all-reduce.1
where the time goes:
time: 212 us
  blocking collectives  97.4 us (46%)
  waiting for transfers between devices  74.3 us (35%)
  matrix products  17.7 us (8%)
  between operations  13.9 us (7%)
  local copies, waits for them, and re-layouts  6.11 us (3%)
  other arithmetic  2.47 us (1%)
    psum x1, waiting for transfers between devices, per_device(): grad_total = lax.psum(grad_part.astype(jnp.bfloat16), 'dp')  66.2 us
    all_to_all x1, blocking collectives, per_device(): lax.all_to_all(input_buffer, 'node', split_axis=0, concat_axis=0, tiled=T...  34.1 us
    all_to_all x1, blocking collectives, send_back(): lax.all_to_all(expert_out, 'node', split_axis=0, concat_axis=0, tiled=True)  33.2 us
    all_to_all x1, blocking collectives, per_device(): lax.all_to_all(grad_buffer, 'node', split_axis=0, concat_axis=0, tiled=True)  30.2 us
    reduce_scatter x1, waiting for transfers between devices, expert_rows(): lax.psum_scatter(partial_value.astype(jnp.bfloat16), 'dev', scatter_dimen...  7.69 us
    dot_general x1, matrix products, per_device(): jnp.einsum('scf,scd->fd', hidden, all_grads, preferred_element_type=jnp.f...  5.59 us
    unnamed x11, local copies, waits for them, and re-layouts  5.32 us
    dot_general x1, matrix products, expert_rows(): jnp.einsum('scd,df->scf', all_inputs, w_gate[0], preferred_element_type=j...  4.25 us
  transfers between devices with their start and end apart: 4, of which 3 were waited for; matrix products, arithmetic and copies ran while one was open for 8% of the time, Pallas kernels for 0%

commit v1 on v0

v1 whole, which is shorter than its diff:
```python
import functools

import jax
import jax.numpy as jnp
from jax import lax
from jax.experimental import pallas as pl
from jax.experimental.pallas import tpu as pltpu
from jax.sharding import PartitionSpec as P

BF = jnp.bfloat16
F32 = jnp.float32
QUARTERS = 4
NODES = 4
PARAMS = pltpu.CompilerParams(vmem_limit_bytes=40 * 1024 * 1024)


def sizes(capacity):
    main = capacity // 16 * 16
    return main, capacity - main


def dot(a, b):
    return jnp.dot(a, b, preferred_element_type=F32)


def iota(shape, dim):
    return lax.broadcasted_iota(jnp.int32, shape, dim)


def slots_of(routes, count):
    rel = routes ^ lax.axis_index("node")
    hits = jnp.where(iota((8, count), 0) == rel, 1.0, 0.0)
    earlier = jnp.where(iota((count, count), 0) < iota((count, count), 1), 1.0, 0.0)
    before = dot(hits.astype(BF), earlier.astype(BF))
    slot = jnp.sum(hits * before, axis=0, keepdims=True).astype(jnp.int32)
    return rel, slot


def codes_of(routes, count, main, rem):
    rel, slot = slots_of(routes, count)
    main_code = jnp.where(slot < main, rel * main + slot, -1)
    rem_code = jnp.where(slot >= main, rel * (QUARTERS * rem) + slot - main, -1000)
    return main_code, rem_code


def fold_kernel(main, rem, scaled, *refs):
    if scaled:
        routes_ref, gates_ref, rows_ref, *outs = refs
    else:
        routes_ref, rows_ref, *outs = refs
    count, width = rows_ref.shape
    piece = width // QUARTERS
    block = QUARTERS * rem
    main_code, rem_code = codes_of(routes_ref[...], count, main, rem)
    main_hot = iota((NODES * main, count), 0) == main_code
    main_mat = jnp.where(main_hot, 1.0, 0.0).astype(BF)
    if scaled:
        main_gate = jnp.sum(jnp.where(main_hot, gates_ref[...], 0.0), axis=1, keepdims=True)
    rest = jnp.zeros((NODES * block, piece), F32)
    for q in range(QUARTERS):
        columns = rows_ref[:, q * piece:(q + 1) * piece]
        value = dot(main_mat, columns)
        rem_hot = iota((NODES * block, count), 0) == rem_code + q * rem
        part = dot(jnp.where(rem_hot, 1.0, 0.0).astype(BF), columns)
        if scaled:
            value = value * main_gate
            part = part * jnp.sum(jnp.where(rem_hot, gates_ref[...], 0.0), axis=1, keepdims=True)
        rest = rest + part
        value = value.astype(BF)
        for p in range(NODES):
            outs[p][q * main:(q + 1) * main, :] = value[p * main:(p + 1) * main]
    rest = rest.astype(BF)
    for p in range(NODES):
        outs[p][QUARTERS * main:, :] = rest[p * block:(p + 1) * block]


def fold(routes_row, rows, gates_row, capacity):
    main, rem = sizes(capacity)
    count, width = rows.shape
    shape = (QUARTERS * capacity, width // QUARTERS)
    scaled = gates_row is not None
    args = (routes_row, gates_row, rows) if scaled else (routes_row, rows)
    return pl.pallas_call(
        functools.partial(fold_kernel, main, rem, scaled),
        out_shape=[jax.ShapeDtypeStruct(shape, BF)] * NODES,
        compiler_params=PARAMS,
        cost_estimate=pl.CostEstimate(flops=2 * count * count * width, bytes_accessed=4 * count * width, transcendentals=0),
    )(*args)


def unfold_matrix(rem, q, groups):
    block = QUARTERS * rem
    r, c = iota((groups * rem, groups * block), 0), iota((groups * rem, groups * block), 1)
    return jnp.where(c == (r // rem) * block + q * rem + r % rem, 1.0, 0.0).astype(BF)


def hidden_kernel(main, rem, *refs):
    folded, (gate_w, up_w, out_ref, gate_acc, up_acc) = refs[:2 * NODES], refs[2 * NODES:]
    q = pl.program_id(0)
    rows = pl.ds(pl.multiple_of(q * main, main), main)
    parts = []
    for h in range(2):
        half = folded[h * NODES:(h + 1) * NODES]
        parts += [ref[rows, :] for ref in half]
        rest = jnp.concatenate([ref[QUARTERS * main:, :] for ref in half], axis=0)
        parts.append(dot(unfold_matrix(rem, q, NODES), rest).astype(BF))
    x = jnp.concatenate(parts, axis=0)
    gate, up = dot(x, gate_w[0]), dot(x, up_w[0])

    @pl.when(q == 0)
    def _():
        gate_acc[...] = gate
        up_acc[...] = up

    @pl.when(q > 0)
    def _():
        gate_acc[...] += gate
        up_acc[...] += up

    @pl.when(q == QUARTERS - 1)
    def _():
        v = gate_acc[...]
        out_ref[...] = (v / (1.0 + jnp.exp(-v)) * up_acc[...]).astype(BF)


def hidden_of(folded, w_gate, w_up, capacity):
    main, rem = sizes(capacity)
    rows, piece = folded[0].shape
    fh = w_gate.shape[2]
    total = 2 * NODES * capacity
    whole = pl.BlockSpec((rows, piece), lambda q: (0, 0))
    weight = pl.BlockSpec((1, piece, fh), lambda q: (0, q, 0))
    return pl.pallas_call(
        functools.partial(hidden_kernel, main, rem),
        grid=(QUARTERS,),
        in_specs=[whole] * (2 * NODES) + [weight, weight],
        out_specs=pl.BlockSpec((total, fh), lambda q: (0, 0)),
        out_shape=jax.ShapeDtypeStruct((total, fh), BF),
        scratch_shapes=[pltpu.VMEM((total, fh), F32)] * 2,
        compiler_params=PARAMS,
        cost_estimate=pl.CostEstimate(flops=4 * total * fh * piece * QUARTERS, bytes_accessed=4 * fh * piece * QUARTERS, transcendentals=total * fh),
    )(*folded, w_gate, w_up)


def down_kernel(main, rem, capacity, hidden_ref, w_ref, own_ref, other_ref):
    q = pl.program_id(0)
    block = QUARTERS * rem
    r, c = iota((NODES * block, NODES * rem), 0), iota((NODES * block, NODES * rem), 1)
    spread = ((r // block) * rem + r % rem == c) & ((r % block) // rem == q)
    spread = jnp.where(spread, 1.0, 0.0).astype(BF)
    for h, out in enumerate((own_ref, other_ref)):
        base = h * NODES * capacity
        top = hidden_ref[base:base + NODES * main, :]
        low = hidden_ref[base + NODES * main:base + NODES * capacity, :]
        low = dot(spread, low).astype(BF)
        value = dot(jnp.concatenate([top, low], axis=0), w_ref[0]).astype(BF)
        for p in range(NODES):
            out[p, pl.ds(pl.multiple_of(q * main, main), main), :] = value[p * main:(p + 1) * main]
            rest = value[NODES * main + p * block:NODES * main + (p + 1) * block]

            @pl.when(q == 0)
            def _():
                out[p, QUARTERS * main:, :] = rest

            @pl.when(q > 0)
            def _():
                out[p, QUARTERS * main:, :] += rest


def down_of(hidden, w_down, capacity):
    main, rem = sizes(capacity)
    fh, width = w_down.shape[1:]
    piece = width // QUARTERS
    shape = (NODES, QUARTERS * capacity, piece)
    out = pl.BlockSpec(shape, lambda q: (0, 0, 0))
    return pl.pallas_call(
        functools.partial(down_kernel, main, rem, capacity),
        grid=(QUARTERS,),
        in_specs=[pl.BlockSpec(hidden.shape, lambda q: (0, 0)), pl.BlockSpec((1, fh, piece), lambda q: (0, 0, q))],
        out_specs=[out, out],
        out_shape=[jax.ShapeDtypeStruct(shape, BF)] * 2,
        compiler_params=PARAMS,
        cost_estimate=pl.CostEstimate(flops=2 * hidden.shape[0] * fh * width, bytes_accessed=2 * fh * width, transcendentals=0),
    )(hidden, w_down)


def add_kernel(a_ref, b_ref, *outs):
    for p, out in enumerate(outs):
        out[...] = (a_ref[p].astype(F32) + b_ref[p].astype(F32)).astype(BF)


def add_parts(a, b):
    return pl.pallas_call(
        add_kernel,
        out_shape=[jax.ShapeDtypeStruct(a.shape[1:], BF)] * a.shape[0],
        compiler_params=PARAMS,
        cost_estimate=pl.CostEstimate(flops=a.size, bytes_accessed=6 * a.size, transcendentals=0),
    )(a, b)


def combine_kernel(main, rem, routes_ref, gates_ref, *refs):
    parts, out_ref = refs[:NODES], refs[NODES]
    count, width = out_ref.shape
    piece = width // QUARTERS
    block = QUARTERS * rem
    main_code, rem_code = codes_of(routes_ref[...], count, main, rem)
    main_hot = jnp.where(iota((NODES * main, count), 0) == main_code, 1.0, 0.0)
    diagonal = iota((count, count), 0) == iota((count, count), 1)
    gate = jnp.sum(jnp.where(diagonal, gates_ref[...], 0.0), axis=1, keepdims=True)
    rest = jnp.concatenate([ref[QUARTERS * main:, :] for ref in parts], axis=0)
    for q in range(QUARTERS):
        rem_hot = jnp.where(iota((NODES * block, count), 0) == rem_code + q * rem, 1.0, 0.0)
        hot = jnp.concatenate([main_hot, rem_hot], axis=0)
        rows = jnp.concatenate([ref[q * main:(q + 1) * main, :] for ref in parts] + [rest], axis=0)
        value = dot(hot.T.astype(BF), rows)
        out_ref[:, q * piece:(q + 1) * piece] = (gate * value).astype(BF)


def combine(routes_row, gates_row, parts, count, width, capacity):
    main, rem = sizes(capacity)
    return pl.pallas_call(
        functools.partial(combine_kernel, main, rem),
        out_shape=jax.ShapeDtypeStruct((count, width), BF),
        compiler_params=PARAMS,
        cost_estimate=pl.CostEstimate(flops=2 * count * count * width, bytes_accessed=4 * count * width, transcendentals=0),
    )(routes_row, gates_row, *parts)


def grad_kernel(main, rem, capacity, groups, *refs):
    hidden = refs[:groups // 2]
    tops, lows = refs[groups // 2:groups // 2 + groups * NODES], refs[groups // 2 + groups * NODES:-1]
    out_ref = refs[-1]
    q = pl.program_id(0)
    half = NODES * capacity
    select = unfold_matrix(rem, q, NODES)
    left, right = [], []
    for g in range(groups):
        h = hidden[g // 2]
        base = g % 2 * half
        left.append(h[base:base + NODES * main, :])
        right += [ref[...] for ref in tops[g * NODES:(g + 1) * NODES]]
    for g in range(groups):
        h = hidden[g // 2]
        base = g % 2 * half
        left.append(h[base + NODES * main:base + half, :])
        rest = jnp.concatenate([ref[...] for ref in lows[g * NODES:(g + 1) * NODES]], axis=0)
        right.append(dot(select, rest).astype(BF))
    left, right = jnp.concatenate(left, axis=0), jnp.concatenate(right, axis=0)
    value = lax.dot_general(left, right, (((0,), (0,)), ((), ())), preferred_element_type=F32)
    out_ref[0] = value.astype(BF)


def gradient(hidden, folded, capacity):
    main, rem = sizes(capacity)
    groups = len(folded) // NODES
    fh = hidden[0].shape[1]
    piece = folded[0].shape[1]
    block = QUARTERS * rem
    low_at = QUARTERS * main // block
    whole = pl.BlockSpec(hidden[0].shape, lambda q: (0, 0))
    top = pl.BlockSpec((main, piece), lambda q: (q, 0))
    low = pl.BlockSpec((block, piece), lambda q: (low_at, 0))
    return pl.pallas_call(
        functools.partial(grad_kernel, main, rem, capacity, groups),
        grid=(QUARTERS,),
        in_specs=[whole] * len(hidden) + [top] * len(folded) + [low] * len(folded),
        out_specs=pl.BlockSpec((1, fh, piece), lambda q: (0, 0, q)),
        out_shape=jax.ShapeDtypeStruct((1, fh, QUARTERS * piece), BF),
        compiler_params=PARAMS,
        cost_estimate=pl.CostEstimate(
            flops=2 * groups * NODES * capacity * fh * piece * QUARTERS,
            bytes_accessed=2 * piece * QUARTERS * (fh + groups * NODES * capacity), transcendentals=0),
    )(*hidden, *folded, *folded)


def by_xor(x, axis, k):
    return lax.ppermute(x, axis, [(i, i ^ k) for i in range(lax.axis_size(axis))])


def per_device(capacity, tokens, cotangent, routes, gates, w_gate, w_up, w_down):
    count, width = tokens.shape
    routes_row, gates_row = routes.reshape(1, count), gates.reshape(1, count)
    t = fold(routes_row, tokens, None, capacity)
    t_in = [t[0]] + [None] * (NODES - 1)
    for p in (3, 2, 1):
        t_in[p] = by_xor(t[p], "node", p)
    w = fold(routes_row, cotangent, gates_row, capacity)
    w_in = [w[0]] + [None] * (NODES - 1)
    for p in (1, 3, 2):
        w_in[p] = by_xor(w[p], "node", p)
    t_other = [by_xor(v, "dev", 1) for v in t_in]
    hidden = hidden_of(t_in + t_other, w_gate, w_up, capacity)
    own, other = down_of(hidden, w_down, capacity)
    results = add_parts(own, by_xor(other, "dev", 1))
    back = [results[0]] + [by_xor(results[p], "node", p) for p in range(1, NODES)]
    mixed_out = combine(routes_row, gates_row, back, count, width, capacity)
    replicas = [w_in, [None] * NODES, [None] * NODES, [None] * NODES]
    for p in range(NODES):
        replicas[1][p], replicas[2][p] = by_xor(w_in[p], "dp", 1), by_xor(w_in[p], "dp", 2)
        replicas[3][p] = by_xor(replicas[1][p], "dp", 2) if p % 2 else by_xor(replicas[2][p], "dp", 1)
    folded = []
    for rows in replicas:
        folded += rows + [by_xor(v, "dev", 1) for v in rows]
    grad = gradient([hidden] + [by_xor(hidden, "dp", k) for k in (1, 2, 3)], folded, capacity)
    return mixed_out, grad


def plain_per_device(capacity, tokens, cotangent, routes, gates, w_gate, w_up, w_down):
    tok_count = tokens.shape[0]
    top_count = routes.shape[1]
    experts = w_gate.shape[0] * lax.axis_size("node")
    flat_routes = routes.reshape(-1)
    hits = (flat_routes[:, None] == jnp.arange(experts, dtype=jnp.int32)[None, :]).astype(jnp.int32)
    before = jnp.cumsum(hits, axis=0) - hits
    target = flat_routes * capacity + jnp.sum(before * hits, axis=1)
    placer = (target[:, None] == jnp.arange(experts * capacity, dtype=jnp.int32)[None, :]).astype(BF)
    token_rows = jnp.repeat(tokens, top_count, axis=0)
    weighted = (gates.reshape(-1)[:, None] * jnp.repeat(cotangent, top_count, axis=0).astype(F32)).astype(BF)
    swap = functools.partial(lax.all_to_all, axis_name="node", split_axis=0, concat_axis=0, tiled=True)
    gather = functools.partial(lax.all_gather, axis_name="dev", axis=0, tiled=True)

    def send(rows):
        placed = jnp.einsum("rs,rd->sd", placer, rows, preferred_element_type=F32).astype(BF)
        return gather(swap(placed.reshape(experts, capacity, -1)))

    all_inputs, all_grads = send(token_rows), send(weighted)
    gate_proj = jnp.einsum("scd,df->scf", all_inputs, w_gate[0], preferred_element_type=F32)
    up_proj = jnp.einsum("scd,df->scf", all_inputs, w_up[0], preferred_element_type=F32)
    hidden = (jax.nn.silu(gate_proj) * up_proj).astype(BF)
    partial_value = jnp.einsum("scf,fd->scd", hidden, w_down[0], preferred_element_type=F32)
    summed = lax.psum_scatter(partial_value.astype(BF), "dev", scatter_dimension=0, tiled=True)
    returned_rows = swap(summed)
    grad_part = jnp.einsum("scf,scd->fd", hidden, all_grads, preferred_element_type=F32)
    grad_total = lax.psum(grad_part.astype(BF), "dp")
    expert_out = jnp.dot(placer, returned_rows.reshape(experts * capacity, -1), preferred_element_type=F32)
    mixed_out = jnp.sum(gates[:, :, None] * expert_out.reshape(tok_count, top_count, -1), axis=1)
    return mixed_out.astype(BF), grad_total[None]


def solution(mesh):
    rows, columns = P(("dp", "node", "dev"), None), P("node", None, "dev")

    def program(tokens, cotangent, routes, gates, w_gate, w_up, w_down):
        nodes, cores, replicas = mesh.shape["node"], mesh.shape["dev"], mesh.shape["dp"]
        count, width = tokens.shape[0] // (nodes * cores * replicas), tokens.shape[1]
        experts = w_gate.shape[0]
        capacity = (count * routes.shape[1] * 9 + 8 * experts - 1) // (8 * experts)
        main, rem = sizes(capacity)
        small = nodes == NODES and replicas == 4 and cores == 2 and experts == nodes and routes.shape[1] == 1
        small = small and main > 0 and rem > 0 and (QUARTERS * rem) % 16 == 0 and main % (QUARTERS * rem) == 0
        small = small and width % (128 * QUARTERS) == 0 and count % 128 == 0
        return jax.shard_map(
            functools.partial(per_device if small else plain_per_device, capacity),
            mesh=mesh,
            in_specs=(rows, rows, rows, rows, columns, columns, P("node", "dev", None)),
            out_specs=(rows, P("node", "dev", None)),
            check_vma=False,
        )(tokens, cotangent, routes, gates, w_gate, w_up, w_down)

    return program
```

time: 212 us -> 141 us (0.67)
  blocking collectives: 97.4 us -> 0 us
  starting transfers between devices: 0.16 us -> 40.8 us
  Pallas kernels: 0 us -> 19.2 us
  matrix products: 17.7 us -> 0 us
  between operations: 13.9 us -> 0.76 us
  waiting for transfers between devices: 74.3 us -> 71.8 us
  other arithmetic: 2.47 us -> 0 us
    all_to_all x3 -> x0, blocking collectives: 97.4 us -> none  [the longest x1 34.1 us: per_device(): lax.all_to_all(input_buffer, 'node', split_axis=0, concat_axis=0, tiled=T...]
    ppermute x0 -> x45, waiting for transfers between devices: none -> 71.8 us  [by_xor(): lax.ppermute(x, axis, [(i, i ^ k) for i in range(lax.axis_size(axis))])]
    psum x1 -> x0, waiting for transfers between devices: 66.2 us -> none  [per_device(): grad_total = lax.psum(grad_part.astype(jnp.bfloat16), 'dp')]
    ppermute x0 -> x45, starting transfers between devices: none -> 40.8 us  [by_xor(): lax.ppermute(x, axis, [(i, i ^ k) for i in range(lax.axis_size(axis))])]
    pallas_call x0 -> x7, Pallas kernels: none -> 19.2 us  [the longest x1 7.9 us: gradient(): pl.pallas_call(functools.partial(grad_kernel, main, rem, capacity, groups...]
    dot_general x7 -> x0, matrix products: 17.7 us -> none  [the longest x1 5.59 us: per_device(): jnp.einsum('scf,scd->fd', hidden, all_grads, preferred_element_type=jnp.f...]
    reduce_scatter x1 -> x0, waiting for transfers between devices: 7.69 us -> none  [expert_rows(): lax.psum_scatter(partial_value.astype(jnp.bfloat16), 'dev', scatter_dimen...]
    unnamed x11 -> x18, local copies, waits for them, and re-layouts: 5.32 us -> 7.75 us
  transfers between devices with their start and end apart: 4 -> 45, of which waited for: 3 -> 12; matrix products, arithmetic and copies ran while one was open for 8% -> 0% of each run, Pallas kernels for 0% -> 12%
where the time goes in v1:
time: 141 us; the launch traced here: 140 us
  waiting for transfers between devices  71.8 us (51%)
  starting transfers between devices  40.8 us (29%)
  Pallas kernels  19.2 us (14%)
  local copies, waits for them, and re-layouts  7.75 us (5%)
    ppermute x45, waiting for transfers between devices, by_xor(): lax.ppermute(x, axis, [(i, i ^ k) for i in range(lax.axis_size(axis))])  71.8 us
    ppermute x45, starting transfers between devices, by_xor(): lax.ppermute(x, axis, [(i, i ^ k) for i in range(lax.axis_size(axis))])  40.8 us
    pallas_call x1, Pallas kernels, gradient(): pl.pallas_call(functools.partial(grad_kernel, main, rem, capacity, groups...  7.9 us
    unnamed x18, local copies, waits for them, and re-layouts  7.75 us
    pallas_call x1, Pallas kernels, down_of(): pl.pallas_call(functools.partial(down_kernel, main, rem, capacity), grid=...  4.16 us
    pallas_call x1, Pallas kernels, hidden_of(): pl.pallas_call(functools.partial(hidden_kernel, main, rem), grid=(QUARTER...  3.94 us
  transfers between devices with their start and end apart: 45, of which 12 were waited for; matrix products, arithmetic and copies ran while one was open for 0% of the time, Pallas kernels for 12%

profile of v1, /device:TPU:0, one launch (start us, length us, event | category | flops | bytes accessed | tf_op | source)
XLA Modules:
  0.0 140.2 jit_solution(7003213865900788344)
XLA Ops:
  0.6 1.2 copy-done.3
  1.8 0.7 copy-done.5
  2.5 0.7 shard_map.86
  3.1 3.1 %collective-permute-start = (bf16[144,896]{1,0:T(8,128)(2,1)S(1)}, bf16[144,896]{1,0:T(8,128)(2,1)S(1)}, u32[]{:S(2)}, u32[]{:S(2)}) collective-permute-start(bf16[144,896]{1,0:T(8,128)(2,1)S(1)} %get-tuple-element.17), channel_id=1, source_target_pairs={{0,2},{2,0},{4,6},{6,4},{1,3},{3,1},{5,7},{7,5},{8,10},{10,8},{12,... | collective-permute-start | bytes 774152 | tf_op jit(solution)/shard_map/ppermute | solution.py:277
  6.2 2.6 %collective-permute-start.1 = (bf16[144,896]{1,0:T(8,128)(2,1)S(1)}, bf16[144,896]{1,0:T(8,128)(2,1)S(1)}, u32[]{:S(2)}, u32[]{:S(2)}) collective-permute-start(bf16[144,896]{1,0:T(8,128)(2,1)S(1)} %get-tuple-element.18), channel_id=1, source_target_pairs={{0,4},{2,6},{4,0},{6,2},{1,5},{3,7},{5,1},{7,3},{8,12},{10,14},{12... | collective-permute-start | bytes 774152 | tf_op jit(solution)/shard_map/ppermute | solution.py:277
  8.8 1.2 copy-done.4
  10.0 0.7 copy-done.7
  10.7 0.7 shard_map.91
  11.4 0.9 collective-permute-start.14
  12.3 5.7 %collective-permute-done.refs_1_ = bf16[144,896]{1,0:T(8,128)(2,1)S(1)} collective-permute-done((bf16[144,896]{1,0:T(8,128)(2,1)S(1)}, bf16[144,896]{1,0:T(8,128)(2,1)S(1)}, u32[]{:S(2)}, u32[]{:S(2)}) %collective-permute-start) | collective-permute-done | bytes 258080 | tf_op jit(solution)/shard_map/ppermute | solution.py:277
  18.0 2.2 %collective-permute-start.15 = (bf16[144,896]{1,0:T(8,128)(2,1)S(1)}, bf16[144,896]{1,0:T(8,128)(2,1)S(1)}, u32[]{:S(2)}, u32[]{:S(2)}) collective-permute-start(bf16[144,896]{1,0:T(8,128)(2,1)S(1)} %get-tuple-element.28), channel_id=1, source_target_pairs={{0,4},{2,6},{4,0},{6,2},{1,5},{3,7},{5,1},{7,3},{8,12},{10,14},{12... | collective-permute-start | bytes 774152 | tf_op jit(solution)/shard_map/ppermute | solution.py:277
  20.2 7.1 %collective-permute-done.1.refs_2_ = bf16[144,896]{1,0:T(8,128)(2,1)S(1)} collective-permute-done((bf16[144,896]{1,0:T(8,128)(2,1)S(1)}, bf16[144,896]{1,0:T(8,128)(2,1)S(1)}, u32[]{:S(2)}, u32[]{:S(2)}) %collective-permute-start.1) | collective-permute-done | bytes 258080 | tf_op jit(solution)/shard_map/ppermute | solution.py:277
  27.4 2.5 %collective-permute-start.16 = (bf16[144,896]{1,0:T(8,128)(2,1)S(1)}, bf16[144,896]{1,0:T(8,128)(2,1)S(1)}, u32[]{:S(2)}, u32[]{:S(2)}) collective-permute-start(bf16[144,896]{1,0:T(8,128)(2,1)S(1)} %get-tuple-element.29), channel_id=1, source_target_pairs={{0,6},{2,4},{4,2},{6,0},{1,7},{3,5},{5,3},{7,1},{8,14},{10,12},{12... | collective-permute-start | bytes 774152 | tf_op jit(solution)/shard_map/ppermute | solution.py:277
  29.8 1.5 %collective-permute-start.29 = (bf16[144,896]{1,0:T(8,128)(2,1)S(1)}, bf16[144,896]{1,0:T(8,128)(2,1)S(1)}, u32[]{:S(2)}, u32[]{:S(2)}) collective-permute-start(bf16[144,896]{1,0:T(8,128)(2,1)S(1)} %get-tuple-element.26.refs_4_.refs_36_), channel_id=1, source_target_pairs={{0,16},{8,24},{16,0},{24,8},{1,17},{9,25},{17,1},{25,9},{2,18},{10... | collective-permute-start | bytes 774152 | tf_op jit(solution)/shard_map/ppermute | solution.py:277
  31.4 1.5 %collective-permute-start.21 = (bf16[144,896]{1,0:T(8,128)(2,1)S(1)}, bf16[144,896]{1,0:T(8,128)(2,1)S(1)}, u32[]{:S(2)}, u32[]{:S(2)}) collective-permute-start(bf16[144,896]{1,0:T(8,128)(2,1)S(1)} %get-tuple-element.26.refs_4_.refs_36_), channel_id=1, source_target_pairs={{0,8},{8,0},{16,24},{24,16},{1,9},{9,1},{17,25},{25,17},{2,10},{10... | collective-permute-start | bytes 774152 | tf_op jit(solution)/shard_map/ppermute | solution.py:277
  32.9 16.6 %collective-permute-done.15.refs_6_.refs_38_ = bf16[144,896]{1,0:T(8,128)(2,1)S(1)} collective-permute-done((bf16[144,896]{1,0:T(8,128)(2,1)S(1)}, bf16[144,896]{1,0:T(8,128)(2,1)S(1)}, u32[]{:S(2)}, u32[]{:S(2)}) %collective-permute-start.15) | collective-permute-done | bytes 258080 | tf_op jit(solution)/shard_map/ppermute | solution.py:277
  49.5 0.5 collective-permute-start.5
  50.1 1.5 %collective-permute-start.30 = (bf16[144,896]{1,0:T(8,128)(2,1)S(1)}, bf16[144,896]{1,0:T(8,128)(2,1)S(1)}, u32[]{:S(2)}, u32[]{:S(2)}) collective-permute-start(bf16[144,896]{1,0:T(8,128)(2,1)S(1)} %collective-permute-done.14.refs_5_.refs_37_), channel_id=1, source_target_pairs={{0,16},{8,24},{16,0},{24,8},{1,17},{9,25},{17,1},{25,9},{2,18},{10... | collective-permute-start | bytes 774152 | tf_op jit(solution)/shard_map/ppermute | solution.py:277
  51.6 1.5 %collective-permute-start.22 = (bf16[144,896]{1,0:T(8,128)(2,1)S(1)}, bf16[144,896]{1,0:T(8,128)(2,1)S(1)}, u32[]{:S(2)}, u32[]{:S(2)}) collective-permute-start(bf16[144,896]{1,0:T(8,128)(2,1)S(1)} %collective-permute-done.14.refs_5_.refs_37_), channel_id=1, source_target_pairs={{0,8},{8,0},{16,24},{24,16},{1,9},{9,1},{17,25},{25,17},{2,10},{10... | collective-permute-start | bytes 774152 | tf_op jit(solution)/shard_map/ppermute | solution.py:277
  53.1 0.6 collective-permute-start.31
  53.7 0.7 collective-permute-start.23
  54.4 4.7 %collective-permute-done.30.refs_21_.refs_53_ = bf16[144,896]{1,0:T(8,128)(2,1)S(1)} collective-permute-done((bf16[144,896]{1,0:T(8,128)(2,1)S(1)}, bf16[144,896]{1,0:T(8,128)(2,1)S(1)}, u32[]{:S(2)}, u32[]{:S(2)}) %collective-permute-start.30) | collective-permute-done | bytes 258080 | tf_op jit(solution)/shard_map/ppermute | solution.py:277
  59.1 1.6 %collective-permute-done.22.refs_13_.refs_45_ = bf16[144,896]{1,0:T(8,128)(2,1)S(1)} collective-permute-done((bf16[144,896]{1,0:T(8,128)(2,1)S(1)}, bf16[144,896]{1,0:T(8,128)(2,1)S(1)}, u32[]{:S(2)}, u32[]{:S(2)}) %collective-permute-start.22) | collective-permute-done | bytes 258080 | tf_op jit(solution)/shard_map/ppermute | solution.py:277
  61.2 2.0 %copy-done = bf16[1,3584,512]{2,1,0:T(8,128)(2,1)S(1)} copy-done((bf16[1,3584,512]{2,1,0:T(8,128)(2,1)S(1)}, bf16[1,3584,512]{2,1,0:T(8,128)(2,1)}, u32[]{:S(2)}) %copy-start) | copy-done | bytes 3670040
  63.2 2.0 %copy-done.1 = bf16[1,3584,512]{2,1,0:T(8,128)(2,1)S(1)} copy-done((bf16[1,3584,512]{2,1,0:T(8,128)(2,1)S(1)}, bf16[1,3584,512]{2,1,0:T(8,128)(2,1)}, u32[]{:S(2)}) %copy-start.1) | copy-done | bytes 3670040
  65.2 3.9 %shard_map.87.hidden_ref.refs_0_ = bf16[288,512]{1,0:T(8,128)(2,1)S(1)} custom-call(bf16[144,896]{1,0:T(8,128)(2,1)S(1)} %get-tuple-element.16.refs_0_, bf16[144,896]{1,0:T(8,128)(2,1)S(1)} %collective-permute-done.refs_1_, bf16[144,896]{1,0:T(8,128)(2,1)S(1)} %collective-permute-done.1.refs_2_, bf16[144,896]{1,0:T(8,128)(2,1)S(1)} %collective-permute-done.2.refs_3_, ...), custom_call_target="tpu_custom_call" | custom-call | flops 2113929216 | bytes 7340032 | tf_op jit(solution)/shard_map/pallas_call | solution.py:133
  69.2 1.6 %collective-permute-start.24 = (bf16[144,896]{1,0:T(8,128)(2,1)S(1)}, bf16[144,896]{1,0:T(8,128)(2,1)S(1)}, u32[]{:S(2)}, u32[]{:S(2)}) collective-permute-start(bf16[144,896]{1,0:T(8,128)(2,1)S(1)} %collective-permute-done.16.refs_7_.refs_39_), channel_id=1, source_target_pairs={{0,8},{8,0},{16,24},{24,16},{1,9},{9,1},{17,25},{25,17},{2,10},{10... | collective-permute-start | bytes 774152 | tf_op jit(solution)/shard_map/ppermute | solution.py:277
  70.8 0.6 collective-permute-start.37
  71.5 4.2 %shard_map.88 = (bf16[4,144,896]{2,1,0:T(8,128)(2,1)S(1)}, bf16[4,144,896]{2,1,0:T(8,128)(2,1)S(1)}) custom-call(bf16[288,512]{1,0:T(8,128)(2,1)S(1)} %shard_map.87.hidden_ref.refs_0_, bf16[1,512,3584]{2,1,0:T(8,128)(2,1)S(1)} %copy-done.2), custom_call_target="tpu_custom_call" | custom-call | flops 1056964608 | bytes 3670016 | tf_op jit(solution)/shard_map/pallas_call | solution.py:176
  76.1 2.2 %collective-permute-done.24.refs_15_.refs_47_ = bf16[144,896]{1,0:T(8,128)(2,1)S(1)} collective-permute-done((bf16[144,896]{1,0:T(8,128)(2,1)S(1)}, bf16[144,896]{1,0:T(8,128)(2,1)S(1)}, u32[]{:S(2)}, u32[]{:S(2)}) %collective-permute-start.24) | collective-permute-done | bytes 258080 | tf_op jit(solution)/shard_map/ppermute | solution.py:277
  78.4 0.5 collective-permute-start.34
  78.9 3.7 %collective-permute-done.37.refs_28_.refs_60_ = bf16[144,896]{1,0:T(8,128)(2,1)S(1)} collective-permute-done((bf16[144,896]{1,0:T(8,128)(2,1)S(1)}, bf16[144,896]{1,0:T(8,128)(2,1)S(1)}, u32[]{:S(2)}, u32[]{:S(2)}) %collective-permute-start.37) | collective-permute-done | bytes 258080 | tf_op jit(solution)/shard_map/ppermute | solution.py:277
  83.1 1.6 %collective-permute-start.39 = (bf16[144,896]{1,0:T(8,128)(2,1)S(1)}, bf16[144,896]{1,0:T(8,128)(2,1)S(1)}, u32[]{:S(2)}, u32[]{:S(2)}) collective-permute-start(bf16[144,896]{1,0:T(8,128)(2,1)S(1)} %collective-permute-done.31.refs_22_.refs_54_), channel_id=1, source_target_pairs={{0,8},{8,0},{16,24},{24,16},{1,9},{9,1},{17,25},{25,17},{2,10},{10... | collective-permute-start | bytes 774152 | tf_op jit(solution)/shard_map/ppermute | solution.py:277
  84.9 4.7 %collective-permute-done.38.refs_29_.refs_61_ = bf16[144,896]{1,0:T(8,128)(2,1)S(1)} collective-permute-done((bf16[144,896]{1,0:T(8,128)(2,1)S(1)}, bf16[144,896]{1,0:T(8,128)(2,1)S(1)}, u32[]{:S(2)}, u32[]{:S(2)}) %collective-permute-start.38) | collective-permute-done | bytes 258080 | tf_op jit(solution)/shard_map/ppermute | solution.py:277
  89.6 0.5 collective-permute-start.36
  90.1 1.7 %collective-permute-done.39.refs_30_.refs_62_ = bf16[144,896]{1,0:T(8,128)(2,1)S(1)} collective-permute-done((bf16[144,896]{1,0:T(8,128)(2,1)S(1)}, bf16[144,896]{1,0:T(8,128)(2,1)S(1)}, u32[]{:S(2)}, u32[]{:S(2)}) %collective-permute-start.39) | collective-permute-done | bytes 258080 | tf_op jit(solution)/shard_map/ppermute | solution.py:277
  91.8 1.5 %collective-permute-start.40 = (bf16[144,896]{1,0:T(8,128)(2,1)S(1)}, bf16[144,896]{1,0:T(8,128)(2,1)S(1)}, u32[]{:S(2)}, u32[]{:S(2)}) collective-permute-start(bf16[144,896]{1,0:T(8,128)(2,1)S(1)} %collective-permute-done.24.refs_15_.refs_47_), channel_id=1, source_target_pairs={{0,16},{8,24},{16,0},{24,8},{1,17},{9,25},{17,1},{25,9},{2,18},{10... | collective-permute-start | bytes 774152 | tf_op jit(solution)/shard_map/ppermute | solution.py:277
  93.3 1.5 %collective-permute-start.13 = (bf16[288,512]{1,0:T(8,128)(2,1)S(1)}, bf16[288,512]{1,0:T(8,128)(2,1)S(1)}, u32[]{:S(2)}, u32[]{:S(2)}) collective-permute-start(bf16[288,512]{1,0:T(8,128)(2,1)S(1)} %shard_map.87.hidden_ref.refs_0_), channel_id=1, source_target_pairs={{0,24},{8,16},{16,8},{24,0},{1,25},{9,17},{17,9},{25,1},{2,26},{10... | collective-permute-start | bytes 884744 | tf_op jit(solution)/shard_map/ppermute | solution.py:277
  95.0 10.9 %collective-permute-done.40.refs_31_.refs_63_ = bf16[144,896]{1,0:T(8,128)(2,1)S(1)} collective-permute-done((bf16[144,896]{1,0:T(8,128)(2,1)S(1)}, bf16[144,896]{1,0:T(8,128)(2,1)S(1)}, u32[]{:S(2)}, u32[]{:S(2)}) %collective-permute-start.40) | collective-permute-done | bytes 258080 | tf_op jit(solution)/shard_map/ppermute | solution.py:277
  105.8 1.5 %collective-permute-start.12 = (bf16[288,512]{1,0:T(8,128)(2,1)S(1)}, bf16[288,512]{1,0:T(8,128)(2,1)S(1)}, u32[]{:S(2)}, u32[]{:S(2)}) collective-permute-start(bf16[288,512]{1,0:T(8,128)(2,1)S(1)} %shard_map.87.hidden_ref.refs_0_), channel_id=1, source_target_pairs={{0,16},{8,24},{16,0},{24,8},{1,17},{9,25},{17,1},{25,9},{2,18},{10... | collective-permute-start | bytes 884744 | tf_op jit(solution)/shard_map/ppermute | solution.py:277
  107.4 1.5 %collective-permute-start.11 = (bf16[288,512]{1,0:T(8,128)(2,1)S(1)}, bf16[288,512]{1,0:T(8,128)(2,1)S(1)}, u32[]{:S(2)}, u32[]{:S(2)}) collective-permute-start(bf16[288,512]{1,0:T(8,128)(2,1)S(1)} %shard_map.87.hidden_ref.refs_0_), channel_id=1, source_target_pairs={{0,8},{8,0},{16,24},{24,16},{1,9},{9,1},{17,25},{25,17},{2,10},{10... | collective-permute-start | bytes 884744 | tf_op jit(solution)/shard_map/ppermute | solution.py:277
  109.7 3.8 %collective-permute-done.12.refs_2_ = bf16[288,512]{1,0:T(8,128)(2,1)S(1)} collective-permute-done((bf16[288,512]{1,0:T(8,128)(2,1)S(1)}, bf16[288,512]{1,0:T(8,128)(2,1)S(1)}, u32[]{:S(2)}, u32[]{:S(2)}) %collective-permute-start.12) | collective-permute-done | bytes 294944 | tf_op jit(solution)/shard_map/ppermute | solution.py:277
  113.5 4.7 %collective-permute-start.8 = (bf16[144,896]{1,0:T(8,128)(2,1)S(1)}, bf16[144,896]{1,0:T(8,128)(2,1)S(1)}, u32[]{:S(2)}, u32[]{:S(2)}) collective-permute-start(bf16[144,896]{1,0:T(8,128)(2,1)S(1)} %get-tuple-element.23), channel_id=1, source_target_pairs={{0,2},{2,0},{4,6},{6,4},{1,3},{3,1},{5,7},{7,5},{8,10},{10,8},{12,... | collective-permute-start | bytes 774152 | tf_op jit(solution)/shard_map/ppermute | solution.py:277
  118.2 2.2 %collective-permute-start.9 = (bf16[144,896]{1,0:T(8,128)(2,1)S(1)}, bf16[144,896]{1,0:T(8,128)(2,1)S(1)}, u32[]{:S(2)}, u32[]{:S(2)}) collective-permute-start(bf16[144,896]{1,0:T(8,128)(2,1)S(1)} %get-tuple-element.24), channel_id=1, source_target_pairs={{0,4},{2,6},{4,0},{6,2},{1,5},{3,7},{5,1},{7,3},{8,12},{10,14},{12... | collective-permute-start | bytes 774152 | tf_op jit(solution)/shard_map/ppermute | solution.py:277
  120.4 1.4 collective-permute-start.10
  121.8 7.9 %shard_map.92 = bf16[1,512,3584]{2,1,0:T(8,128)(2,1)} custom-call(bf16[288,512]{1,0:T(8,128)(2,1)S(1)} %shard_map.87.hidden_ref.refs_0_, bf16[288,512]{1,0:T(8,128)(2,1)S(1)} %collective-permute-done.11.refs_1_, bf16[288,512]{1,0:T(8,128)(2,1)S(1)} %collective-permute-done.12.refs_2_, bf16[288,512]{1,0:T(8,128)(2,1)S(1)} %collective-permute-done.13.refs_3_, ...), custom_call_target="tpu_custom_call" | custom-call | flops 4227858432 | bytes 11927552 | tf_op jit(solution)/shard_map/pallas_call | solution.py:263
  129.7 8.9 %collective-permute-done.9.refs_2_ = bf16[144,896]{1,0:T(8,128)(2,1)S(1)} collective-permute-done((bf16[144,896]{1,0:T(8,128)(2,1)S(1)}, bf16[144,896]{1,0:T(8,128)(2,1)S(1)}, u32[]{:S(2)}, u32[]{:S(2)}) %collective-permute-start.9) | collective-permute-done | bytes 258080 | tf_op jit(solution)/shard_map/ppermute | solution.py:277
  138.6 1.6 %shard_map.90 = bf16[128,3584]{1,0:T(8,128)(2,1)} custom-call(s32[1,128]{1,0:T(1,128)S(1)} %bitcast.4, f32[1,128]{1,0:T(1,128)S(1)} %bitcast.6, bf16[144,896]{1,0:T(8,128)(2,1)S(1)} %get-tuple-element.22.refs_0_, bf16[144,896]{1,0:T(8,128)(2,1)S(1)} %collective-permute-done.8.refs_1_, bf16[144,896]{1,0:T(8,128)(2,1)S(1)} %collective-permute-done.9.refs_2_, ...), custom_call_target="tpu_custom_call" | custom-call | flops 117440512 | bytes 1835008 | tf_op jit(solution)/shard_map/pallas_call | solution.py:221
  (67 shorter events, 2.9 us)
Async XLA Ops:
  3.1 14.9 %collective-permute-start = (bf16[144,896]{1,0:T(8,128)(2,1)S(1)}, bf16[144,896]{1,0:T(8,128)(2,1)S(1)}, u32[]{:S(2)}, u32[]{:S(2)}) collective-permute-start(bf16[144,896]{1,0:T(8,128)(2,1)S(1)} %get-tuple-element.17), channel_id=1, source_target_pairs={{0,2},{2,0},{4,6},{6,4},{1,3},{3,1},{5,7},{7,5},{8,10},{10,8},{12,... | collective-permute-start | bytes 774152 | tf_op jit(solution)/shard_map/ppermute | solution.py:277
  6.2 21.1 %collective-permute-start.1 = (bf16[144,896]{1,0:T(8,128)(2,1)S(1)}, bf16[144,896]{1,0:T(8,128)(2,1)S(1)}, u32[]{:S(2)}, u32[]{:S(2)}) collective-permute-start(bf16[144,896]{1,0:T(8,128)(2,1)S(1)} %get-tuple-element.18), channel_id=1, source_target_pairs={{0,4},{2,6},{4,0},{6,2},{1,5},{3,7},{5,1},{7,3},{8,12},{10,14},{12... | collective-permute-start | bytes 774152 | tf_op jit(solution)/shard_map/ppermute | solution.py:277
  8.8 21.0 %collective-permute-start.2 = (bf16[144,896]{1,0:T(8,128)(2,1)S(1)}, bf16[144,896]{1,0:T(8,128)(2,1)S(1)}, u32[]{:S(2)}, u32[]{:S(2)}) collective-permute-start(bf16[144,896]{1,0:T(8,128)(2,1)S(1)} %get-tuple-element.19), channel_id=1, source_target_pairs={{0,6},{2,4},{4,2},{6,0},{1,7},{3,5},{5,3},{7,1},{8,14},{10,12},{12... | collective-permute-start | bytes 774152 | tf_op jit(solution)/shard_map/ppermute | solution.py:277
  8.8 22.5 %collective-permute-start.3 = (bf16[144,896]{1,0:T(8,128)(2,1)S(1)}, bf16[144,896]{1,0:T(8,128)(2,1)S(1)}, u32[]{:S(2)}, u32[]{:S(2)}) collective-permute-start(bf16[144,896]{1,0:T(8,128)(2,1)S(1)} %get-tuple-element.16.refs_0_), channel_id=1, source_target_pairs={{0,1},{1,0},{2,3},{3,2},{4,5},{5,4},{6,7},{7,6},{8,9},{9,8},{10,11... | collective-permute-start | bytes 774152 | tf_op jit(solution)/shard_map/ppermute | solution.py:277
  11.4 21.5 %collective-permute-start.14 = (bf16[144,896]{1,0:T(8,128)(2,1)S(1)}, bf16[144,896]{1,0:T(8,128)(2,1)S(1)}, u32[]{:S(2)}, u32[]{:S(2)}) collective-permute-start(bf16[144,896]{1,0:T(8,128)(2,1)S(1)} %get-tuple-element.27), channel_id=1, source_target_pairs={{0,2},{2,0},{4,6},{6,4},{1,3},{3,1},{5,7},{7,5},{8,10},{10,8},{12,... | collective-permute-start | bytes 774152 | tf_op jit(solution)/shard_map/ppermute | solution.py:277
  18.0 31.4 %collective-permute-start.15 = (bf16[144,896]{1,0:T(8,128)(2,1)S(1)}, bf16[144,896]{1,0:T(8,128)(2,1)S(1)}, u32[]{:S(2)}, u32[]{:S(2)}) collective-permute-start(bf16[144,896]{1,0:T(8,128)(2,1)S(1)} %get-tuple-element.28), channel_id=1, source_target_pairs={{0,4},{2,6},{4,0},{6,2},{1,5},{3,7},{5,1},{7,3},{8,12},{10,14},{12... | collective-permute-start | bytes 774152 | tf_op jit(solution)/shard_map/ppermute | solution.py:277
  27.4 22.1 %collective-permute-start.16 = (bf16[144,896]{1,0:T(8,128)(2,1)S(1)}, bf16[144,896]{1,0:T(8,128)(2,1)S(1)}, u32[]{:S(2)}, u32[]{:S(2)}) collective-permute-start(bf16[144,896]{1,0:T(8,128)(2,1)S(1)} %get-tuple-element.29), channel_id=1, source_target_pairs={{0,6},{2,4},{4,2},{6,0},{1,7},{3,5},{5,3},{7,1},{8,14},{10,12},{12... | collective-permute-start | bytes 774152 | tf_op jit(solution)/shard_map/ppermute | solution.py:277
  29.8 20.1 %collective-permute-start.29 = (bf16[144,896]{1,0:T(8,128)(2,1)S(1)}, bf16[144,896]{1,0:T(8,128)(2,1)S(1)}, u32[]{:S(2)}, u32[]{:S(2)}) collective-permute-start(bf16[144,896]{1,0:T(8,128)(2,1)S(1)} %get-tuple-element.26.refs_4_.refs_36_), channel_id=1, source_target_pairs={{0,16},{8,24},{16,0},{24,8},{1,17},{9,25},{17,1},{25,9},{2,18},{10... | collective-permute-start | bytes 774152 | tf_op jit(solution)/shard_map/ppermute | solution.py:277
  31.4 18.7 %collective-permute-start.21 = (bf16[144,896]{1,0:T(8,128)(2,1)S(1)}, bf16[144,896]{1,0:T(8,128)(2,1)S(1)}, u32[]{:S(2)}, u32[]{:S(2)}) collective-permute-start(bf16[144,896]{1,0:T(8,128)(2,1)S(1)} %get-tuple-element.26.refs_4_.refs_36_), channel_id=1, source_target_pairs={{0,8},{8,0},{16,24},{24,16},{1,9},{9,1},{17,25},{25,17},{2,10},{10... | collective-permute-start | bytes 774152 | tf_op jit(solution)/shard_map/ppermute | solution.py:277
  32.9 18.7 %collective-permute-start.17 = (bf16[144,896]{1,0:T(8,128)(2,1)S(1)}, bf16[144,896]{1,0:T(8,128)(2,1)S(1)}, u32[]{:S(2)}, u32[]{:S(2)}) collective-permute-start(bf16[144,896]{1,0:T(8,128)(2,1)S(1)} %get-tuple-element.26.refs_4_.refs_36_), channel_id=1, source_target_pairs={{0,1},{1,0},{2,3},{3,2},{4,5},{5,4},{6,7},{7,6},{8,9},{9,8},{10,11... | collective-permute-start | bytes 774152 | tf_op jit(solution)/shard_map/ppermute | solution.py:277
  49.5 3.6 %collective-permute-start.4 = (bf16[144,896]{1,0:T(8,128)(2,1)S(1)}, bf16[144,896]{1,0:T(8,128)(2,1)S(1)}, u32[]{:S(2)}, u32[]{:S(2)}) collective-permute-start(bf16[144,896]{1,0:T(8,128)(2,1)S(1)} %collective-permute-done.refs_1_), channel_id=1, source_target_pairs={{0,1},{1,0},{2,3},{3,2},{4,5},{5,4},{6,7},{7,6},{8,9},{9,8},{10,11... | collective-permute-start | bytes 774152 | tf_op jit(solution)/shard_map/ppermute | solution.py:277
  49.5 3.6 %collective-permute-start.5 = (bf16[144,896]{1,0:T(8,128)(2,1)S(1)}, bf16[144,896]{1,0:T(8,128)(2,1)S(1)}, u32[]{:S(2)}, u32[]{:S(2)}) collective-permute-start(bf16[144,896]{1,0:T(8,128)(2,1)S(1)} %collective-permute-done.1.refs_2_), channel_id=1, source_target_pairs={{0,1},{1,0},{2,3},{3,2},{4,5},{5,4},{6,7},{7,6},{8,9},{9,8},{10,11... | collective-permute-start | bytes 774152 | tf_op jit(solution)/shard_map/ppermute | solution.py:277
  50.0 3.7 %collective-permute-start.6 = (bf16[144,896]{1,0:T(8,128)(2,1)S(1)}, bf16[144,896]{1,0:T(8,128)(2,1)S(1)}, u32[]{:S(2)}, u32[]{:S(2)}) collective-permute-start(bf16[144,896]{1,0:T(8,128)(2,1)S(1)} %collective-permute-done.2.refs_3_), channel_id=1, source_target_pairs={{0,1},{1,0},{2,3},{3,2},{4,5},{5,4},{6,7},{7,6},{8,9},{9,8},{10,11... | collective-permute-start | bytes 774152 | tf_op jit(solution)/shard_map/ppermute | solution.py:277
  50.1 9.0 %collective-permute-start.30 = (bf16[144,896]{1,0:T(8,128)(2,1)S(1)}, bf16[144,896]{1,0:T(8,128)(2,1)S(1)}, u32[]{:S(2)}, u32[]{:S(2)}) collective-permute-start(bf16[144,896]{1,0:T(8,128)(2,1)S(1)} %collective-permute-done.14.refs_5_.refs_37_), channel_id=1, source_target_pairs={{0,16},{8,24},{16,0},{24,8},{1,17},{9,25},{17,1},{25,9},{2,18},{10... | collective-permute-start | bytes 774152 | tf_op jit(solution)/shard_map/ppermute | solution.py:277
  51.6 9.1 %collective-permute-start.22 = (bf16[144,896]{1,0:T(8,128)(2,1)S(1)}, bf16[144,896]{1,0:T(8,128)(2,1)S(1)}, u32[]{:S(2)}, u32[]{:S(2)}) collective-permute-start(bf16[144,896]{1,0:T(8,128)(2,1)S(1)} %collective-permute-done.14.refs_5_.refs_37_), channel_id=1, source_target_pairs={{0,8},{8,0},{16,24},{24,16},{1,9},{9,1},{17,25},{25,17},{2,10},{10... | collective-permute-start | bytes 774152 | tf_op jit(solution)/shard_map/ppermute | solution.py:277
  53.1 16.1 %collective-permute-start.18 = (bf16[144,896]{1,0:T(8,128)(2,1)S(1)}, bf16[144,896]{1,0:T(8,128)(2,1)S(1)}, u32[]{:S(2)}, u32[]{:S(2)}) collective-permute-start(bf16[144,896]{1,0:T(8,128)(2,1)S(1)} %collective-permute-done.14.refs_5_.refs_37_), channel_id=1, source_target_pairs={{0,1},{1,0},{2,3},{3,2},{4,5},{5,4},{6,7},{7,6},{8,9},{9,8},{10,11... | collective-permute-start | bytes 774152 | tf_op jit(solution)/shard_map/ppermute | solution.py:277
  53.1 17.7 %collective-permute-start.31 = (bf16[144,896]{1,0:T(8,128)(2,1)S(1)}, bf16[144,896]{1,0:T(8,128)(2,1)S(1)}, u32[]{:S(2)}, u32[]{:S(2)}) collective-permute-start(bf16[144,896]{1,0:T(8,128)(2,1)S(1)} %collective-permute-done.15.refs_6_.refs_38_), channel_id=1, source_target_pairs={{0,16},{8,24},{16,0},{24,8},{1,17},{9,25},{17,1},{25,9},{2,18},{10... | collective-permute-start | bytes 774152 | tf_op jit(solution)/shard_map/ppermute | solution.py:277
  53.7 17.1 %collective-permute-start.23 = (bf16[144,896]{1,0:T(8,128)(2,1)S(1)}, bf16[144,896]{1,0:T(8,128)(2,1)S(1)}, u32[]{:S(2)}, u32[]{:S(2)}) collective-permute-start(bf16[144,896]{1,0:T(8,128)(2,1)S(1)} %collective-permute-done.15.refs_6_.refs_38_), channel_id=1, source_target_pairs={{0,8},{8,0},{16,24},{24,16},{1,9},{9,1},{17,25},{25,17},{2,10},{10... | collective-permute-start | bytes 774152 | tf_op jit(solution)/shard_map/ppermute | solution.py:277
  59.1 12.3 %collective-permute-start.19 = (bf16[144,896]{1,0:T(8,128)(2,1)S(1)}, bf16[144,896]{1,0:T(8,128)(2,1)S(1)}, u32[]{:S(2)}, u32[]{:S(2)}) collective-permute-start(bf16[144,896]{1,0:T(8,128)(2,1)S(1)} %collective-permute-done.15.refs_6_.refs_38_), channel_id=1, source_target_pairs={{0,1},{1,0},{2,3},{3,2},{4,5},{5,4},{6,7},{7,6},{8,9},{9,8},{10,11... | collective-permute-start | bytes 774152 | tf_op jit(solution)/shard_map/ppermute | solution.py:277
  60.7 15.0 %collective-permute-start.32 = (bf16[144,896]{1,0:T(8,128)(2,1)S(1)}, bf16[144,896]{1,0:T(8,128)(2,1)S(1)}, u32[]{:S(2)}, u32[]{:S(2)}) collective-permute-start(bf16[144,896]{1,0:T(8,128)(2,1)S(1)} %collective-permute-done.16.refs_7_.refs_39_), channel_id=1, source_target_pairs={{0,16},{8,24},{16,0},{24,8},{1,17},{9,25},{17,1},{25,9},{2,18},{10... | collective-permute-start | bytes 774152 | tf_op jit(solution)/shard_map/ppermute | solution.py:277
  65.2 6.3 %copy-start.2 = (bf16[1,512,3584]{2,1,0:T(8,128)(2,1)S(1)}, bf16[1,512,3584]{2,1,0:T(8,128)(2,1)}, u32[]{:S(2)}) copy-start(bf16[1,512,3584]{2,1,0:T(8,128)(2,1)} %w_ref.1) | copy-start | bytes 11010052
  69.2 9.2 %collective-permute-start.24 = (bf16[144,896]{1,0:T(8,128)(2,1)S(1)}, bf16[144,896]{1,0:T(8,128)(2,1)S(1)}, u32[]{:S(2)}, u32[]{:S(2)}) collective-permute-start(bf16[144,896]{1,0:T(8,128)(2,1)S(1)} %collective-permute-done.16.refs_7_.refs_39_), channel_id=1, source_target_pairs={{0,8},{8,0},{16,24},{24,16},{1,9},{9,1},{17,25},{25,17},{2,10},{10... | collective-permute-start | bytes 774152 | tf_op jit(solution)/shard_map/ppermute | solution.py:277
  70.8 7.6 %collective-permute-start.20 = (bf16[144,896]{1,0:T(8,128)(2,1)S(1)}, bf16[144,896]{1,0:T(8,128)(2,1)S(1)}, u32[]{:S(2)}, u32[]{:S(2)}) collective-permute-start(bf16[144,896]{1,0:T(8,128)(2,1)S(1)} %collective-permute-done.16.refs_7_.refs_39_), channel_id=1, source_target_pairs={{0,1},{1,0},{2,3},{3,2},{4,5},{5,4},{6,7},{7,6},{8,9},{9,8},{10,11... | collective-permute-start | bytes 774152 | tf_op jit(solution)/shard_map/ppermute | solution.py:277
  70.8 11.8 %collective-permute-start.37 = (bf16[144,896]{1,0:T(8,128)(2,1)S(1)}, bf16[144,896]{1,0:T(8,128)(2,1)S(1)}, u32[]{:S(2)}, u32[]{:S(2)}) collective-permute-start(bf16[144,896]{1,0:T(8,128)(2,1)S(1)} %collective-permute-done.29.refs_20_.refs_52_), channel_id=1, source_target_pairs={{0,8},{8,0},{16,24},{24,16},{1,9},{9,1},{17,25},{25,17},{2,10},{10... | collective-permute-start | bytes 774152 | tf_op jit(solution)/shard_map/ppermute | solution.py:277
  71.4 11.7 %collective-permute-start.33 = (bf16[144,896]{1,0:T(8,128)(2,1)S(1)}, bf16[144,896]{1,0:T(8,128)(2,1)S(1)}, u32[]{:S(2)}, u32[]{:S(2)}) collective-permute-start(bf16[144,896]{1,0:T(8,128)(2,1)S(1)} %collective-permute-done.29.refs_20_.refs_52_), channel_id=1, source_target_pairs={{0,1},{1,0},{2,3},{3,2},{4,5},{5,4},{6,7},{7,6},{8,9},{9,8},{10,11... | collective-permute-start | bytes 774152 | tf_op jit(solution)/shard_map/ppermute | solution.py:277
  75.7 33.7 %collective-permute-start.7 = (bf16[4,144,896]{2,1,0:T(8,128)(2,1)S(1)}, bf16[4,144,896]{2,1,0:T(8,128)(2,1)S(1)}, u32[]{:S(2)}, u32[]{:S(2)}) collective-permute-start(bf16[4,144,896]{2,1,0:T(8,128)(2,1)S(1)} %get-tuple-element.21), channel_id=1, source_target_pairs={{0,1},{1,0},{2,3},{3,2},{4,5},{5,4},{6,7},{7,6},{8,9},{9,8},{10,11... | collective-permute-start | bytes 3096584 | tf_op jit(solution)/shard_map/ppermute | solution.py:277
  78.4 4.7 %collective-permute-start.25 = (bf16[144,896]{1,0:T(8,128)(2,1)S(1)}, bf16[144,896]{1,0:T(8,128)(2,1)S(1)}, u32[]{:S(2)}, u32[]{:S(2)}) collective-permute-start(bf16[144,896]{1,0:T(8,128)(2,1)S(1)} %collective-permute-done.21.refs_12_.refs_44_), channel_id=1, source_target_pairs={{0,1},{1,0},{2,3},{3,2},{4,5},{5,4},{6,7},{7,6},{8,9},{9,8},{10,11... | collective-permute-start | bytes 774152 | tf_op jit(solution)/shard_map/ppermute | solution.py:277
  78.4 6.3 %collective-permute-start.34 = (bf16[144,896]{1,0:T(8,128)(2,1)S(1)}, bf16[144,896]{1,0:T(8,128)(2,1)S(1)}, u32[]{:S(2)}, u32[]{:S(2)}) collective-permute-start(bf16[144,896]{1,0:T(8,128)(2,1)S(1)} %collective-permute-done.30.refs_21_.refs_53_), channel_id=1, source_target_pairs={{0,1},{1,0},{2,3},{3,2},{4,5},{5,4},{6,7},{7,6},{8,9},{9,8},{10,11... | collective-permute-start | bytes 774152 | tf_op jit(solution)/shard_map/ppermute | solution.py:277
  82.6 6.9 %collective-permute-start.38 = (bf16[144,896]{1,0:T(8,128)(2,1)S(1)}, bf16[144,896]{1,0:T(8,128)(2,1)S(1)}, u32[]{:S(2)}, u32[]{:S(2)}) collective-permute-start(bf16[144,896]{1,0:T(8,128)(2,1)S(1)} %collective-permute-done.22.refs_13_.refs_45_), channel_id=1, source_target_pairs={{0,16},{8,24},{16,0},{24,8},{1,17},{9,25},{17,1},{25,9},{2,18},{10... | collective-permute-start | bytes 774152 | tf_op jit(solution)/shard_map/ppermute | solution.py:277
  83.1 6.4 %collective-permute-start.26 = (bf16[144,896]{1,0:T(8,128)(2,1)S(1)}, bf16[144,896]{1,0:T(8,128)(2,1)S(1)}, u32[]{:S(2)}, u32[]{:S(2)}) collective-permute-start(bf16[144,896]{1,0:T(8,128)(2,1)S(1)} %collective-permute-done.22.refs_13_.refs_45_), channel_id=1, source_target_pairs={{0,1},{1,0},{2,3},{3,2},{4,5},{5,4},{6,7},{7,6},{8,9},{9,8},{10,11... | collective-permute-start | bytes 774152 | tf_op jit(solution)/shard_map/ppermute | solution.py:277
  83.1 8.6 %collective-permute-start.39 = (bf16[144,896]{1,0:T(8,128)(2,1)S(1)}, bf16[144,896]{1,0:T(8,128)(2,1)S(1)}, u32[]{:S(2)}, u32[]{:S(2)}) collective-permute-start(bf16[144,896]{1,0:T(8,128)(2,1)S(1)} %collective-permute-done.31.refs_22_.refs_54_), channel_id=1, source_target_pairs={{0,8},{8,0},{16,24},{24,16},{1,9},{9,1},{17,25},{25,17},{2,10},{10... | collective-permute-start | bytes 774152 | tf_op jit(solution)/shard_map/ppermute | solution.py:277
  84.7 8.6 %collective-permute-start.35 = (bf16[144,896]{1,0:T(8,128)(2,1)S(1)}, bf16[144,896]{1,0:T(8,128)(2,1)S(1)}, u32[]{:S(2)}, u32[]{:S(2)}) collective-permute-start(bf16[144,896]{1,0:T(8,128)(2,1)S(1)} %collective-permute-done.31.refs_22_.refs_54_), channel_id=1, source_target_pairs={{0,1},{1,0},{2,3},{3,2},{4,5},{5,4},{6,7},{7,6},{8,9},{9,8},{10,11... | collective-permute-start | bytes 774152 | tf_op jit(solution)/shard_map/ppermute | solution.py:277
  89.6 3.7 %collective-permute-start.27 = (bf16[144,896]{1,0:T(8,128)(2,1)S(1)}, bf16[144,896]{1,0:T(8,128)(2,1)S(1)}, u32[]{:S(2)}, u32[]{:S(2)}) collective-permute-start(bf16[144,896]{1,0:T(8,128)(2,1)S(1)} %collective-permute-done.23.refs_14_.refs_46_), channel_id=1, source_target_pairs={{0,1},{1,0},{2,3},{3,2},{4,5},{5,4},{6,7},{7,6},{8,9},{9,8},{10,11... | collective-permute-start | bytes 774152 | tf_op jit(solution)/shard_map/ppermute | solution.py:277
  89.6 5.2 %collective-permute-start.36 = (bf16[144,896]{1,0:T(8,128)(2,1)S(1)}, bf16[144,896]{1,0:T(8,128)(2,1)S(1)}, u32[]{:S(2)}, u32[]{:S(2)}) collective-permute-start(bf16[144,896]{1,0:T(8,128)(2,1)S(1)} %collective-permute-done.32.refs_23_.refs_55_), channel_id=1, source_target_pairs={{0,1},{1,0},{2,3},{3,2},{4,5},{5,4},{6,7},{7,6},{8,9},{9,8},{10,11... | collective-permute-start | bytes 774152 | tf_op jit(solution)/shard_map/ppermute | solution.py:277
  91.8 14.1 %collective-permute-start.40 = (bf16[144,896]{1,0:T(8,128)(2,1)S(1)}, bf16[144,896]{1,0:T(8,128)(2,1)S(1)}, u32[]{:S(2)}, u32[]{:S(2)}) collective-permute-start(bf16[144,896]{1,0:T(8,128)(2,1)S(1)} %collective-permute-done.24.refs_15_.refs_47_), channel_id=1, source_target_pairs={{0,16},{8,24},{16,0},{24,8},{1,17},{9,25},{17,1},{25,9},{2,18},{10... | collective-permute-start | bytes 774152 | tf_op jit(solution)/shard_map/ppermute | solution.py:277
  93.3 14.1 %collective-permute-start.28 = (bf16[144,896]{1,0:T(8,128)(2,1)S(1)}, bf16[144,896]{1,0:T(8,128)(2,1)S(1)}, u32[]{:S(2)}, u32[]{:S(2)}) collective-permute-start(bf16[144,896]{1,0:T(8,128)(2,1)S(1)} %collective-permute-done.24.refs_15_.refs_47_), channel_id=1, source_target_pairs={{0,1},{1,0},{2,3},{3,2},{4,5},{5,4},{6,7},{7,6},{8,9},{9,8},{10,11... | collective-permute-start | bytes 774152 | tf_op jit(solution)/shard_map/ppermute | solution.py:277
  93.3 15.6 %collective-permute-start.13 = (bf16[288,512]{1,0:T(8,128)(2,1)S(1)}, bf16[288,512]{1,0:T(8,128)(2,1)S(1)}, u32[]{:S(2)}, u32[]{:S(2)}) collective-permute-start(bf16[288,512]{1,0:T(8,128)(2,1)S(1)} %shard_map.87.hidden_ref.refs_0_), channel_id=1, source_target_pairs={{0,24},{8,16},{16,8},{24,0},{1,25},{9,17},{17,9},{25,1},{2,26},{10... | collective-permute-start | bytes 884744 | tf_op jit(solution)/shard_map/ppermute | solution.py:277
  94.8 14.1 %collective-permute-start.41 = (bf16[144,896]{1,0:T(8,128)(2,1)S(1)}, bf16[144,896]{1,0:T(8,128)(2,1)S(1)}, u32[]{:S(2)}, u32[]{:S(2)}) collective-permute-start(bf16[144,896]{1,0:T(8,128)(2,1)S(1)} %collective-permute-done.37.refs_28_.refs_60_), channel_id=1, source_target_pairs={{0,1},{1,0},{2,3},{3,2},{4,5},{5,4},{6,7},{7,6},{8,9},{9,8},{10,11... | collective-permute-start | bytes 774152 | tf_op jit(solution)/shard_map/ppermute | solution.py:277
  105.8 7.7 %collective-permute-start.12 = (bf16[288,512]{1,0:T(8,128)(2,1)S(1)}, bf16[288,512]{1,0:T(8,128)(2,1)S(1)}, u32[]{:S(2)}, u32[]{:S(2)}) collective-permute-start(bf16[288,512]{1,0:T(8,128)(2,1)S(1)} %shard_map.87.hidden_ref.refs_0_), channel_id=1, source_target_pairs={{0,16},{8,24},{16,0},{24,8},{1,17},{9,25},{17,1},{25,9},{2,18},{10... | collective-permute-start | bytes 884744 | tf_op jit(solution)/shard_map/ppermute | solution.py:277
  107.4 10.8 %collective-permute-start.11 = (bf16[288,512]{1,0:T(8,128)(2,1)S(1)}, bf16[288,512]{1,0:T(8,128)(2,1)S(1)}, u32[]{:S(2)}, u32[]{:S(2)}) collective-permute-start(bf16[288,512]{1,0:T(8,128)(2,1)S(1)} %shard_map.87.hidden_ref.refs_0_), channel_id=1, source_target_pairs={{0,8},{8,0},{16,24},{24,16},{1,9},{9,1},{17,25},{25,17},{2,10},{10... | collective-permute-start | bytes 884744 | tf_op jit(solution)/shard_map/ppermute | solution.py:277
  108.9 11.6 %collective-permute-start.42 = (bf16[144,896]{1,0:T(8,128)(2,1)S(1)}, bf16[144,896]{1,0:T(8,128)(2,1)S(1)}, u32[]{:S(2)}, u32[]{:S(2)}) collective-permute-start(bf16[144,896]{1,0:T(8,128)(2,1)S(1)} %collective-permute-done.38.refs_29_.refs_61_), channel_id=1, source_target_pairs={{0,1},{1,0},{2,3},{3,2},{4,5},{5,4},{6,7},{7,6},{8,9},{9,8},{10,11... | collective-permute-start | bytes 774152 | tf_op jit(solution)/shard_map/ppermute | solution.py:277
  108.9 12.9 %collective-permute-start.43 = (bf16[144,896]{1,0:T(8,128)(2,1)S(1)}, bf16[144,896]{1,0:T(8,128)(2,1)S(1)}, u32[]{:S(2)}, u32[]{:S(2)}) collective-permute-start(bf16[144,896]{1,0:T(8,128)(2,1)S(1)} %collective-permute-done.39.refs_30_.refs_62_), channel_id=1, source_target_pairs={{0,1},{1,0},{2,3},{3,2},{4,5},{5,4},{6,7},{7,6},{8,9},{9,8},{10,11... | collective-permute-start | bytes 774152 | tf_op jit(solution)/shard_map/ppermute | solution.py:277
  109.4 12.4 %collective-permute-start.44 = (bf16[144,896]{1,0:T(8,128)(2,1)S(1)}, bf16[144,896]{1,0:T(8,128)(2,1)S(1)}, u32[]{:S(2)}, u32[]{:S(2)}) collective-permute-start(bf16[144,896]{1,0:T(8,128)(2,1)S(1)} %collective-permute-done.40.refs_31_.refs_63_), channel_id=1, source_target_pairs={{0,1},{1,0},{2,3},{3,2},{4,5},{5,4},{6,7},{7,6},{8,9},{9,8},{10,11... | collective-permute-start | bytes 774152 | tf_op jit(solution)/shard_map/ppermute | solution.py:277
  113.5 16.2 %collective-permute-start.8 = (bf16[144,896]{1,0:T(8,128)(2,1)S(1)}, bf16[144,896]{1,0:T(8,128)(2,1)S(1)}, u32[]{:S(2)}, u32[]{:S(2)}) collective-permute-start(bf16[144,896]{1,0:T(8,128)(2,1)S(1)} %get-tuple-element.23), channel_id=1, source_target_pairs={{0,2},{2,0},{4,6},{6,4},{1,3},{3,1},{5,7},{7,5},{8,10},{10,8},{12,... | collective-permute-start | bytes 774152 | tf_op jit(solution)/shard_map/ppermute | solution.py:277
  118.2 20.4 %collective-permute-start.9 = (bf16[144,896]{1,0:T(8,128)(2,1)S(1)}, bf16[144,896]{1,0:T(8,128)(2,1)S(1)}, u32[]{:S(2)}, u32[]{:S(2)}) collective-permute-start(bf16[144,896]{1,0:T(8,128)(2,1)S(1)} %get-tuple-element.24), channel_id=1, source_target_pairs={{0,4},{2,6},{4,0},{6,2},{1,5},{3,7},{5,1},{7,3},{8,12},{10,14},{12... | collective-permute-start | bytes 774152 | tf_op jit(solution)/shard_map/ppermute | solution.py:277
  120.4 18.2 %copy-start.6 = (s32[128,1]{0,1:T(1,128)S(1)}, s32[128,1]{0,1:T(1,128)}, u32[]{:S(2)}) copy-start(s32[128,1]{0,1:T(1,128)} %param.9) | copy-start | bytes 1540
  120.4 18.2 %copy-start.8 = (f32[128,1]{0,1:T(1,128)S(1)}, f32[128,1]{0,1:T(1,128)}, u32[]{:S(2)}) copy-start(f32[128,1]{0,1:T(1,128)} %param.10) | copy-start | bytes 1540
  120.4 18.2 %collective-permute-start.10 = (bf16[144,896]{1,0:T(8,128)(2,1)S(1)}, bf16[144,896]{1,0:T(8,128)(2,1)S(1)}, u32[]{:S(2)}, u32[]{:S(2)}) collective-permute-start(bf16[144,896]{1,0:T(8,128)(2,1)S(1)} %get-tuple-element.25), channel_id=1, source_target_pairs={{0,6},{2,4},{4,2},{6,0},{1,7},{3,5},{5,3},{7,1},{8,14},{10,12},{12... | collective-permute-start | bytes 774152 | tf_op jit(solution)/shard_map/ppermute | solution.py:277
  (6 other events, 7.7 us)

commit v2 on v1

--- a/solution.py
+++ b/solution.py
@@ -277,6 +277,10 @@
     return lax.ppermute(x, axis, [(i, i ^ k) for i in range(lax.axis_size(axis))])
 
 
+def after(x, *earlier):
+    return lax.optimization_barrier((x, *earlier))[0]
+
+
 def per_device(capacity, tokens, cotangent, routes, gates, w_gate, w_up, w_down):
     count, width = tokens.shape
     routes_row, gates_row = routes.reshape(1, count), gates.reshape(1, count)
@@ -285,14 +289,15 @@
     for p in (3, 2, 1):
         t_in[p] = by_xor(t[p], "node", p)
     w = fold(routes_row, cotangent, gates_row, capacity)
-    w_in = [w[0]] + [None] * (NODES - 1)
-    for p in (1, 3, 2):
-        w_in[p] = by_xor(w[p], "node", p)
+    w_in = [w[0], by_xor(w[1], "node", 1), None, None]
+    w_in[3] = by_xor(after(w[3], t_in[3], t_in[2]), "node", 3)
+    w_in[2] = by_xor(after(w[2], w_in[3]), "node", 2)
     t_other = [by_xor(v, "dev", 1) for v in t_in]
     hidden = hidden_of(t_in + t_other, w_gate, w_up, capacity)
     own, other = down_of(hidden, w_down, capacity)
     results = add_parts(own, by_xor(other, "dev", 1))
-    back = [results[0]] + [by_xor(results[p], "node", p) for p in range(1, NODES)]
+    back = [results[0], by_xor(results[1], "node", 1)]
+    back += [by_xor(after(results[p], w_in[2]), "node", p) for p in (2, 3)]
     mixed_out = combine(routes_row, gates_row, back, count, width, capacity)
     replicas = [w_in, [None] * NODES, [None] * NODES, [None] * NODES]
     for p in range(NODES):

time: 141 us -> 123 us (0.87)
  waiting for transfers between devices: 71.8 us -> 55.5 us
    ppermute x45, waiting for transfers between devices: 71.8 us -> 55.5 us  [by_xor(): lax.ppermute(x, axis, [(i, i ^ k) for i in range(lax.axis_size(axis))])]
  transfers between devices with their start and end apart: 45 -> 45, of which waited for: 12 -> 15; matrix products, arithmetic and copies ran while one was open for 0% -> 0% of each run, Pallas kernels for 12% -> 14%
where the time goes in v2:
time: 123 us
  waiting for transfers between devices  55.5 us (45%)
  starting transfers between devices  39.7 us (32%)
  Pallas kernels  19.2 us (16%)
  local copies, waits for them, and re-layouts  7.75 us (6%)
    ppermute x45, waiting for transfers between devices, by_xor(): lax.ppermute(x, axis, [(i, i ^ k) for i in range(lax.axis_size(axis))])  55.5 us
    ppermute x45, starting transfers between devices, by_xor(): lax.ppermute(x, axis, [(i, i ^ k) for i in range(lax.axis_size(axis))])  39.7 us
    pallas_call x1, Pallas kernels, gradient(): pl.pallas_call(functools.partial(grad_kernel, main, rem, capacity, groups...  7.89 us
    unnamed x18, local copies, waits for them, and re-layouts  7.75 us
    pallas_call x1, Pallas kernels, down_of(): pl.pallas_call(functools.partial(down_kernel, main, rem, capacity), grid=...  4.16 us
    pallas_call x1, Pallas kernels, hidden_of(): pl.pallas_call(functools.partial(hidden_kernel, main, rem), grid=(QUARTER...  3.93 us
  transfers between devices with their start and end apart: 45, of which 15 were waited for; matrix products, arithmetic and copies ran while one was open for 0% of the time, Pallas kernels for 14%

profile of v2, /device:TPU:0, one launch (start us, length us, event | category | flops | bytes accessed | tf_op | source)
XLA Modules:
  0.0 122.8 jit_solution(8667967309113277382)
XLA Ops:
  0.6 1.2 copy-done.3
  1.8 0.7 copy-done.5
  2.5 0.7 shard_map.86
  3.1 3.1 %collective-permute-start = (bf16[144,896]{1,0:T(8,128)(2,1)S(1)}, bf16[144,896]{1,0:T(8,128)(2,1)S(1)}, u32[]{:S(2)}, u32[]{:S(2)}) collective-permute-start(bf16[144,896]{1,0:T(8,128)(2,1)S(1)} %get-tuple-element.21), channel_id=1, source_target_pairs={{0,2},{2,0},{4,6},{6,4},{1,3},{3,1},{5,7},{7,5},{8,10},{10,8},{12,... | collective-permute-start | bytes 774152 | tf_op jit(solution)/shard_map/ppermute | solution.py:277
  6.2 2.6 %collective-permute-start.1 = (bf16[144,896]{1,0:T(8,128)(2,1)S(1)}, bf16[144,896]{1,0:T(8,128)(2,1)S(1)}, u32[]{:S(2)}, u32[]{:S(2)}) collective-permute-start(bf16[144,896]{1,0:T(8,128)(2,1)S(1)} %get-tuple-element.22), channel_id=1, source_target_pairs={{0,4},{2,6},{4,0},{6,2},{1,5},{3,7},{5,1},{7,3},{8,12},{10,14},{12... | collective-permute-start | bytes 774152 | tf_op jit(solution)/shard_map/ppermute | solution.py:277
  8.8 1.2 copy-done.4
  10.0 0.7 copy-done.7
  10.7 0.7 shard_map.90
  11.4 0.9 collective-permute-start.16
  12.3 5.7 %collective-permute-done.refs_1_ = bf16[144,896]{1,0:T(8,128)(2,1)S(1)} collective-permute-done((bf16[144,896]{1,0:T(8,128)(2,1)S(1)}, bf16[144,896]{1,0:T(8,128)(2,1)S(1)}, u32[]{:S(2)}, u32[]{:S(2)}) %collective-permute-start) | collective-permute-done | bytes 258080 | tf_op jit(solution)/shard_map/ppermute | solution.py:277
  18.0 2.0 %collective-permute-start.29 = (bf16[144,896]{1,0:T(8,128)(2,1)S(1)}, bf16[144,896]{1,0:T(8,128)(2,1)S(1)}, u32[]{:S(2)}, u32[]{:S(2)}) collective-permute-start(bf16[144,896]{1,0:T(8,128)(2,1)S(1)} %get-tuple-element.36.refs_4_.refs_36_), channel_id=1, source_target_pairs={{0,16},{8,24},{16,0},{24,8},{1,17},{9,25},{17,1},{25,9},{2,18},{10... | collective-permute-start | bytes 774152 | tf_op jit(solution)/shard_map/ppermute | solution.py:277
  20.0 7.3 %collective-permute-done.1.refs_2_ = bf16[144,896]{1,0:T(8,128)(2,1)S(1)} collective-permute-done((bf16[144,896]{1,0:T(8,128)(2,1)S(1)}, bf16[144,896]{1,0:T(8,128)(2,1)S(1)}, u32[]{:S(2)}, u32[]{:S(2)}) %collective-permute-start.1) | collective-permute-done | bytes 258080 | tf_op jit(solution)/shard_map/ppermute | solution.py:277
  27.4 1.5 %collective-permute-start.21 = (bf16[144,896]{1,0:T(8,128)(2,1)S(1)}, bf16[144,896]{1,0:T(8,128)(2,1)S(1)}, u32[]{:S(2)}, u32[]{:S(2)}) collective-permute-start(bf16[144,896]{1,0:T(8,128)(2,1)S(1)} %get-tuple-element.36.refs_4_.refs_36_), channel_id=1, source_target_pairs={{0,8},{8,0},{16,24},{24,16},{1,9},{9,1},{17,25},{25,17},{2,10},{10... | collective-permute-start | bytes 774152 | tf_op jit(solution)/shard_map/ppermute | solution.py:277
  29.4 3.4 %collective-permute-start.9 = (bf16[144,896]{1,0:T(8,128)(2,1)S(1)}, bf16[144,896]{1,0:T(8,128)(2,1)S(1)}, u32[]{:S(2)}, u32[]{:S(2)}) collective-permute-start(bf16[144,896]{1,0:T(8,128)(2,1)S(1)} %get-tuple-element.31), channel_id=1, source_target_pairs={{0,6},{2,4},{4,2},{6,0},{1,7},{3,5},{5,3},{7,1},{8,14},{10,12},{12... | collective-permute-start | bytes 774152 | tf_op jit(solution)/shard_map/ppermute | solution.py:277
  32.8 0.9 collective-permute-done.21.refs_12_.refs_44_
  33.7 1.5 %collective-permute-start.30 = (bf16[144,896]{1,0:T(8,128)(2,1)S(1)}, bf16[144,896]{1,0:T(8,128)(2,1)S(1)}, u32[]{:S(2)}, u32[]{:S(2)}) collective-permute-start(bf16[144,896]{1,0:T(8,128)(2,1)S(1)} %collective-permute-done.16.refs_5_.refs_37_), channel_id=1, source_target_pairs={{0,16},{8,24},{16,0},{24,8},{1,17},{9,25},{17,1},{25,9},{2,18},{10... | collective-permute-start | bytes 774152 | tf_op jit(solution)/shard_map/ppermute | solution.py:277
  35.2 1.5 %collective-permute-start.22 = (bf16[144,896]{1,0:T(8,128)(2,1)S(1)}, bf16[144,896]{1,0:T(8,128)(2,1)S(1)}, u32[]{:S(2)}, u32[]{:S(2)}) collective-permute-start(bf16[144,896]{1,0:T(8,128)(2,1)S(1)} %collective-permute-done.16.refs_5_.refs_37_), channel_id=1, source_target_pairs={{0,8},{8,0},{16,24},{24,16},{1,9},{9,1},{17,25},{25,17},{2,10},{10... | collective-permute-start | bytes 774152 | tf_op jit(solution)/shard_map/ppermute | solution.py:277
  36.7 2.8 %collective-permute-done.9.refs_7_.refs_39_ = bf16[144,896]{1,0:T(8,128)(2,1)S(1)} collective-permute-done((bf16[144,896]{1,0:T(8,128)(2,1)S(1)}, bf16[144,896]{1,0:T(8,128)(2,1)S(1)}, u32[]{:S(2)}, u32[]{:S(2)}) %collective-permute-start.9) | collective-permute-done | bytes 258080 | tf_op jit(solution)/shard_map/ppermute | solution.py:277
  39.5 0.5 collective-permute-start.37
  40.2 2.1 %collective-permute-done.30.refs_21_.refs_53_ = bf16[144,896]{1,0:T(8,128)(2,1)S(1)} collective-permute-done((bf16[144,896]{1,0:T(8,128)(2,1)S(1)}, bf16[144,896]{1,0:T(8,128)(2,1)S(1)}, u32[]{:S(2)}, u32[]{:S(2)}) %collective-permute-start.30) | collective-permute-done | bytes 258080 | tf_op jit(solution)/shard_map/ppermute | solution.py:277
  42.3 2.0 %collective-permute-done.22.refs_13_.refs_45_ = bf16[144,896]{1,0:T(8,128)(2,1)S(1)} collective-permute-done((bf16[144,896]{1,0:T(8,128)(2,1)S(1)}, bf16[144,896]{1,0:T(8,128)(2,1)S(1)}, u32[]{:S(2)}, u32[]{:S(2)}) %collective-permute-start.22) | collective-permute-done | bytes 258080 | tf_op jit(solution)/shard_map/ppermute | solution.py:277
  44.3 4.1 %collective-permute-start.10 = (bf16[144,896]{1,0:T(8,128)(2,1)S(1)}, bf16[144,896]{1,0:T(8,128)(2,1)S(1)}, u32[]{:S(2)}, u32[]{:S(2)}) collective-permute-start(bf16[144,896]{1,0:T(8,128)(2,1)S(1)} %get-tuple-element.32), channel_id=1, source_target_pairs={{0,4},{2,6},{4,0},{6,2},{1,5},{3,7},{5,1},{7,3},{8,12},{10,14},{12... | collective-permute-start | bytes 774152 | tf_op jit(solution)/shard_map/ppermute | solution.py:277
  48.4 1.5 %collective-permute-start.32 = (bf16[144,896]{1,0:T(8,128)(2,1)S(1)}, bf16[144,896]{1,0:T(8,128)(2,1)S(1)}, u32[]{:S(2)}, u32[]{:S(2)}) collective-permute-start(bf16[144,896]{1,0:T(8,128)(2,1)S(1)} %collective-permute-done.9.refs_7_.refs_39_), channel_id=1, source_target_pairs={{0,16},{8,24},{16,0},{24,8},{1,17},{9,25},{17,1},{25,9},{2,18},{10... | collective-permute-start | bytes 774152 | tf_op jit(solution)/shard_map/ppermute | solution.py:277
  49.9 2.0 %copy-done = bf16[1,3584,512]{2,1,0:T(8,128)(2,1)S(1)} copy-done((bf16[1,3584,512]{2,1,0:T(8,128)(2,1)S(1)}, bf16[1,3584,512]{2,1,0:T(8,128)(2,1)}, u32[]{:S(2)}) %copy-start) | copy-done | bytes 3670040
  51.9 2.0 %copy-done.1 = bf16[1,3584,512]{2,1,0:T(8,128)(2,1)S(1)} copy-done((bf16[1,3584,512]{2,1,0:T(8,128)(2,1)S(1)}, bf16[1,3584,512]{2,1,0:T(8,128)(2,1)}, u32[]{:S(2)}) %copy-start.1) | copy-done | bytes 3670040
  54.0 3.9 %shard_map.87.hidden_ref.refs_0_ = bf16[288,512]{1,0:T(8,128)(2,1)S(1)} custom-call(bf16[144,896]{1,0:T(8,128)(2,1)S(1)} %get-tuple-element.20.refs_0_, bf16[144,896]{1,0:T(8,128)(2,1)S(1)} %collective-permute-done.refs_1_, bf16[144,896]{1,0:T(8,128)(2,1)S(1)} %collective-permute-done.1.refs_2_, bf16[144,896]{1,0:T(8,128)(2,1)S(1)} %collective-permute-done.2.refs_3_, ...), custom_call_target="tpu_custom_call" | custom-call | flops 2113929216 | bytes 7340032 | tf_op jit(solution)/shard_map/pallas_call | solution.py:133
  57.9 0.8 collective-permute-start.24
  59.2 1.3 %collective-permute-done.10.refs_6_.refs_38_ = bf16[144,896]{1,0:T(8,128)(2,1)S(1)} collective-permute-done((bf16[144,896]{1,0:T(8,128)(2,1)S(1)}, bf16[144,896]{1,0:T(8,128)(2,1)S(1)}, u32[]{:S(2)}, u32[]{:S(2)}) %collective-permute-start.10) | collective-permute-done | bytes 258080 | tf_op jit(solution)/shard_map/ppermute | solution.py:277
  60.5 1.5 %collective-permute-start.38 = (bf16[144,896]{1,0:T(8,128)(2,1)S(1)}, bf16[144,896]{1,0:T(8,128)(2,1)S(1)}, u32[]{:S(2)}, u32[]{:S(2)}) collective-permute-start(bf16[144,896]{1,0:T(8,128)(2,1)S(1)} %collective-permute-done.22.refs_13_.refs_45_), channel_id=1, source_target_pairs={{0,16},{8,24},{16,0},{24,8},{1,17},{9,25},{17,1},{25,9},{2,18},{10... | collective-permute-start | bytes 774152 | tf_op jit(solution)/shard_map/ppermute | solution.py:277
  62.0 4.2 %shard_map.88 = (bf16[4,144,896]{2,1,0:T(8,128)(2,1)S(1)}, bf16[4,144,896]{2,1,0:T(8,128)(2,1)S(1)}) custom-call(bf16[288,512]{1,0:T(8,128)(2,1)S(1)} %shard_map.87.hidden_ref.refs_0_, bf16[1,512,3584]{2,1,0:T(8,128)(2,1)S(1)} %copy-done.2), custom_call_target="tpu_custom_call" | custom-call | flops 1056964608 | bytes 3670016 | tf_op jit(solution)/shard_map/pallas_call | solution.py:176
  66.8 0.6 collective-permute-start.15
  67.4 1.5 %collective-permute-start.14 = (bf16[288,512]{1,0:T(8,128)(2,1)S(1)}, bf16[288,512]{1,0:T(8,128)(2,1)S(1)}, u32[]{:S(2)}, u32[]{:S(2)}) collective-permute-start(bf16[288,512]{1,0:T(8,128)(2,1)S(1)} %shard_map.87.hidden_ref.refs_0_), channel_id=1, source_target_pairs={{0,16},{8,24},{16,0},{24,8},{1,17},{9,25},{17,1},{25,9},{2,18},{10... | collective-permute-start | bytes 884744 | tf_op jit(solution)/shard_map/ppermute | solution.py:277
  69.3 1.1 collective-permute-start.13
  70.4 1.1 collective-permute-start.31
  71.5 6.1 %collective-permute-done.15.refs_3_ = bf16[288,512]{1,0:T(8,128)(2,1)S(1)} collective-permute-done((bf16[288,512]{1,0:T(8,128)(2,1)S(1)}, bf16[288,512]{1,0:T(8,128)(2,1)S(1)}, u32[]{:S(2)}, u32[]{:S(2)}) %collective-permute-start.15) | collective-permute-done | bytes 294944 | tf_op jit(solution)/shard_map/ppermute | solution.py:277
  77.6 0.7 collective-permute-start.23
  78.3 4.9 %collective-permute-done.14.refs_2_ = bf16[288,512]{1,0:T(8,128)(2,1)S(1)} collective-permute-done((bf16[288,512]{1,0:T(8,128)(2,1)S(1)}, bf16[288,512]{1,0:T(8,128)(2,1)S(1)}, u32[]{:S(2)}, u32[]{:S(2)}) %collective-permute-start.14) | collective-permute-done | bytes 294944 | tf_op jit(solution)/shard_map/ppermute | solution.py:277
  83.6 4.3 %collective-permute-done.31.refs_22_.refs_54_ = bf16[144,896]{1,0:T(8,128)(2,1)S(1)} collective-permute-done((bf16[144,896]{1,0:T(8,128)(2,1)S(1)}, bf16[144,896]{1,0:T(8,128)(2,1)S(1)}, u32[]{:S(2)}, u32[]{:S(2)}) %collective-permute-start.31) | collective-permute-done | bytes 258080 | tf_op jit(solution)/shard_map/ppermute | solution.py:277
  88.0 1.0 collective-permute-start.40
  89.0 0.8 collective-permute-start.39
  90.0 5.6 %collective-permute-done.40.refs_31_.refs_63_ = bf16[144,896]{1,0:T(8,128)(2,1)S(1)} collective-permute-done((bf16[144,896]{1,0:T(8,128)(2,1)S(1)}, bf16[144,896]{1,0:T(8,128)(2,1)S(1)}, u32[]{:S(2)}, u32[]{:S(2)}) %collective-permute-start.40) | collective-permute-done | bytes 258080 | tf_op jit(solution)/shard_map/ppermute | solution.py:277
  95.5 0.5 collective-permute-start.27
  96.0 1.6 %collective-permute-done.39.refs_30_.refs_62_ = bf16[144,896]{1,0:T(8,128)(2,1)S(1)} collective-permute-done((bf16[144,896]{1,0:T(8,128)(2,1)S(1)}, bf16[144,896]{1,0:T(8,128)(2,1)S(1)}, u32[]{:S(2)}, u32[]{:S(2)}) %collective-permute-start.39) | collective-permute-done | bytes 258080 | tf_op jit(solution)/shard_map/ppermute | solution.py:277
  98.4 0.6 collective-permute-start.12
  99.1 3.8 %collective-permute-start.8 = (bf16[144,896]{1,0:T(8,128)(2,1)S(1)}, bf16[144,896]{1,0:T(8,128)(2,1)S(1)}, u32[]{:S(2)}, u32[]{:S(2)}) collective-permute-start(bf16[144,896]{1,0:T(8,128)(2,1)S(1)} %get-tuple-element.27), channel_id=1, source_target_pairs={{0,2},{2,0},{4,6},{6,4},{1,3},{3,1},{5,7},{7,5},{8,10},{10,8},{12,... | collective-permute-start | bytes 774152 | tf_op jit(solution)/shard_map/ppermute | solution.py:277
  102.9 7.9 %shard_map.92 = bf16[1,512,3584]{2,1,0:T(8,128)(2,1)} custom-call(bf16[288,512]{1,0:T(8,128)(2,1)S(1)} %shard_map.87.hidden_ref.refs_0_, bf16[288,512]{1,0:T(8,128)(2,1)S(1)} %collective-permute-done.13.refs_1_, bf16[288,512]{1,0:T(8,128)(2,1)S(1)} %collective-permute-done.14.refs_2_, bf16[288,512]{1,0:T(8,128)(2,1)S(1)} %collective-permute-done.15.refs_3_, ...), custom_call_target="tpu_custom_call" | custom-call | flops 4227858432 | bytes 11927552 | tf_op jit(solution)/shard_map/pallas_call | solution.py:263
  110.8 10.5 %collective-permute-done.11.refs_2_ = bf16[144,896]{1,0:T(8,128)(2,1)S(1)} collective-permute-done((bf16[144,896]{1,0:T(8,128)(2,1)S(1)}, bf16[144,896]{1,0:T(8,128)(2,1)S(1)}, u32[]{:S(2)}, u32[]{:S(2)}) %collective-permute-start.11) | collective-permute-done | bytes 258080 | tf_op jit(solution)/shard_map/ppermute | solution.py:277
  121.3 1.6 %shard_map.91 = bf16[128,3584]{1,0:T(8,128)(2,1)} custom-call(s32[1,128]{1,0:T(1,128)S(1)} %bitcast.4, f32[1,128]{1,0:T(1,128)S(1)} %bitcast.6, bf16[144,896]{1,0:T(8,128)(2,1)S(1)} %get-tuple-element.26.refs_0_, bf16[144,896]{1,0:T(8,128)(2,1)S(1)} %collective-permute-done.8.refs_1_, bf16[144,896]{1,0:T(8,128)(2,1)S(1)} %collective-permute-done.11.refs_2_, ...), custom_call_target="tpu_custom_call" | custom-call | flops 117440512 | bytes 1835008 | tf_op jit(solution)/shard_map/pallas_call | solution.py:221
  (67 shorter events, 3.8 us)
Async XLA Ops:
  3.1 14.9 %collective-permute-start = (bf16[144,896]{1,0:T(8,128)(2,1)S(1)}, bf16[144,896]{1,0:T(8,128)(2,1)S(1)}, u32[]{:S(2)}, u32[]{:S(2)}) collective-permute-start(bf16[144,896]{1,0:T(8,128)(2,1)S(1)} %get-tuple-element.21), channel_id=1, source_target_pairs={{0,2},{2,0},{4,6},{6,4},{1,3},{3,1},{5,7},{7,5},{8,10},{10,8},{12,... | collective-permute-start | bytes 774152 | tf_op jit(solution)/shard_map/ppermute | solution.py:277
  6.2 21.1 %collective-permute-start.1 = (bf16[144,896]{1,0:T(8,128)(2,1)S(1)}, bf16[144,896]{1,0:T(8,128)(2,1)S(1)}, u32[]{:S(2)}, u32[]{:S(2)}) collective-permute-start(bf16[144,896]{1,0:T(8,128)(2,1)S(1)} %get-tuple-element.22), channel_id=1, source_target_pairs={{0,4},{2,6},{4,0},{6,2},{1,5},{3,7},{5,1},{7,3},{8,12},{10,14},{12... | collective-permute-start | bytes 774152 | tf_op jit(solution)/shard_map/ppermute | solution.py:277
  8.8 20.0 %collective-permute-start.2 = (bf16[144,896]{1,0:T(8,128)(2,1)S(1)}, bf16[144,896]{1,0:T(8,128)(2,1)S(1)}, u32[]{:S(2)}, u32[]{:S(2)}) collective-permute-start(bf16[144,896]{1,0:T(8,128)(2,1)S(1)} %get-tuple-element.23), channel_id=1, source_target_pairs={{0,6},{2,4},{4,2},{6,0},{1,7},{3,5},{5,3},{7,1},{8,14},{10,12},{12... | collective-permute-start | bytes 774152 | tf_op jit(solution)/shard_map/ppermute | solution.py:277
  8.8 20.1 %collective-permute-start.3 = (bf16[144,896]{1,0:T(8,128)(2,1)S(1)}, bf16[144,896]{1,0:T(8,128)(2,1)S(1)}, u32[]{:S(2)}, u32[]{:S(2)}) collective-permute-start(bf16[144,896]{1,0:T(8,128)(2,1)S(1)} %get-tuple-element.20.refs_0_), channel_id=1, source_target_pairs={{0,1},{1,0},{2,3},{3,2},{4,5},{5,4},{6,7},{7,6},{8,9},{9,8},{10,11... | collective-permute-start | bytes 774152 | tf_op jit(solution)/shard_map/ppermute | solution.py:277
  11.4 18.0 %collective-permute-start.16 = (bf16[144,896]{1,0:T(8,128)(2,1)S(1)}, bf16[144,896]{1,0:T(8,128)(2,1)S(1)}, u32[]{:S(2)}, u32[]{:S(2)}) collective-permute-start(bf16[144,896]{1,0:T(8,128)(2,1)S(1)} %get-tuple-element.37), channel_id=1, source_target_pairs={{0,2},{2,0},{4,6},{6,4},{1,3},{3,1},{5,7},{7,5},{8,10},{10,8},{12,... | collective-permute-start | bytes 774152 | tf_op jit(solution)/shard_map/ppermute | solution.py:277
  18.0 14.8 %collective-permute-start.29 = (bf16[144,896]{1,0:T(8,128)(2,1)S(1)}, bf16[144,896]{1,0:T(8,128)(2,1)S(1)}, u32[]{:S(2)}, u32[]{:S(2)}) collective-permute-start(bf16[144,896]{1,0:T(8,128)(2,1)S(1)} %get-tuple-element.36.refs_4_.refs_36_), channel_id=1, source_target_pairs={{0,16},{8,24},{16,0},{24,8},{1,17},{9,25},{17,1},{25,9},{2,18},{10... | collective-permute-start | bytes 774152 | tf_op jit(solution)/shard_map/ppermute | solution.py:277
  27.4 6.3 %collective-permute-start.21 = (bf16[144,896]{1,0:T(8,128)(2,1)S(1)}, bf16[144,896]{1,0:T(8,128)(2,1)S(1)}, u32[]{:S(2)}, u32[]{:S(2)}) collective-permute-start(bf16[144,896]{1,0:T(8,128)(2,1)S(1)} %get-tuple-element.36.refs_4_.refs_36_), channel_id=1, source_target_pairs={{0,8},{8,0},{16,24},{24,16},{1,9},{9,1},{17,25},{25,17},{2,10},{10... | collective-permute-start | bytes 774152 | tf_op jit(solution)/shard_map/ppermute | solution.py:277
  28.9 4.8 %collective-permute-start.17 = (bf16[144,896]{1,0:T(8,128)(2,1)S(1)}, bf16[144,896]{1,0:T(8,128)(2,1)S(1)}, u32[]{:S(2)}, u32[]{:S(2)}) collective-permute-start(bf16[144,896]{1,0:T(8,128)(2,1)S(1)} %get-tuple-element.36.refs_4_.refs_36_), channel_id=1, source_target_pairs={{0,1},{1,0},{2,3},{3,2},{4,5},{5,4},{6,7},{7,6},{8,9},{9,8},{10,11... | collective-permute-start | bytes 774152 | tf_op jit(solution)/shard_map/ppermute | solution.py:277
  28.9 6.4 %collective-permute-start.4 = (bf16[144,896]{1,0:T(8,128)(2,1)S(1)}, bf16[144,896]{1,0:T(8,128)(2,1)S(1)}, u32[]{:S(2)}, u32[]{:S(2)}) collective-permute-start(bf16[144,896]{1,0:T(8,128)(2,1)S(1)} %collective-permute-done.refs_1_), channel_id=1, source_target_pairs={{0,1},{1,0},{2,3},{3,2},{4,5},{5,4},{6,7},{7,6},{8,9},{9,8},{10,11... | collective-permute-start | bytes 774152 | tf_op jit(solution)/shard_map/ppermute | solution.py:277
  29.4 10.1 %collective-permute-start.9 = (bf16[144,896]{1,0:T(8,128)(2,1)S(1)}, bf16[144,896]{1,0:T(8,128)(2,1)S(1)}, u32[]{:S(2)}, u32[]{:S(2)}) collective-permute-start(bf16[144,896]{1,0:T(8,128)(2,1)S(1)} %get-tuple-element.31), channel_id=1, source_target_pairs={{0,6},{2,4},{4,2},{6,0},{1,7},{3,5},{5,3},{7,1},{8,14},{10,12},{12... | collective-permute-start | bytes 774152 | tf_op jit(solution)/shard_map/ppermute | solution.py:277
  32.8 6.7 %collective-permute-start.5 = (bf16[144,896]{1,0:T(8,128)(2,1)S(1)}, bf16[144,896]{1,0:T(8,128)(2,1)S(1)}, u32[]{:S(2)}, u32[]{:S(2)}) collective-permute-start(bf16[144,896]{1,0:T(8,128)(2,1)S(1)} %collective-permute-done.1.refs_2_), channel_id=1, source_target_pairs={{0,1},{1,0},{2,3},{3,2},{4,5},{5,4},{6,7},{7,6},{8,9},{9,8},{10,11... | collective-permute-start | bytes 774152 | tf_op jit(solution)/shard_map/ppermute | solution.py:277
  33.7 6.3 %collective-permute-start.6 = (bf16[144,896]{1,0:T(8,128)(2,1)S(1)}, bf16[144,896]{1,0:T(8,128)(2,1)S(1)}, u32[]{:S(2)}, u32[]{:S(2)}) collective-permute-start(bf16[144,896]{1,0:T(8,128)(2,1)S(1)} %collective-permute-done.2.refs_3_), channel_id=1, source_target_pairs={{0,1},{1,0},{2,3},{3,2},{4,5},{5,4},{6,7},{7,6},{8,9},{9,8},{10,11... | collective-permute-start | bytes 774152 | tf_op jit(solution)/shard_map/ppermute | solution.py:277
  33.7 8.6 %collective-permute-start.30 = (bf16[144,896]{1,0:T(8,128)(2,1)S(1)}, bf16[144,896]{1,0:T(8,128)(2,1)S(1)}, u32[]{:S(2)}, u32[]{:S(2)}) collective-permute-start(bf16[144,896]{1,0:T(8,128)(2,1)S(1)} %collective-permute-done.16.refs_5_.refs_37_), channel_id=1, source_target_pairs={{0,16},{8,24},{16,0},{24,8},{1,17},{9,25},{17,1},{25,9},{2,18},{10... | collective-permute-start | bytes 774152 | tf_op jit(solution)/shard_map/ppermute | solution.py:277
  35.2 9.1 %collective-permute-start.22 = (bf16[144,896]{1,0:T(8,128)(2,1)S(1)}, bf16[144,896]{1,0:T(8,128)(2,1)S(1)}, u32[]{:S(2)}, u32[]{:S(2)}) collective-permute-start(bf16[144,896]{1,0:T(8,128)(2,1)S(1)} %collective-permute-done.16.refs_5_.refs_37_), channel_id=1, source_target_pairs={{0,8},{8,0},{16,24},{24,16},{1,9},{9,1},{17,25},{25,17},{2,10},{10... | collective-permute-start | bytes 774152 | tf_op jit(solution)/shard_map/ppermute | solution.py:277
  39.5 8.9 %collective-permute-start.18 = (bf16[144,896]{1,0:T(8,128)(2,1)S(1)}, bf16[144,896]{1,0:T(8,128)(2,1)S(1)}, u32[]{:S(2)}, u32[]{:S(2)}) collective-permute-start(bf16[144,896]{1,0:T(8,128)(2,1)S(1)} %collective-permute-done.16.refs_5_.refs_37_), channel_id=1, source_target_pairs={{0,1},{1,0},{2,3},{3,2},{4,5},{5,4},{6,7},{7,6},{8,9},{9,8},{10,11... | collective-permute-start | bytes 774152 | tf_op jit(solution)/shard_map/ppermute | solution.py:277
  39.5 18.4 %collective-permute-start.37 = (bf16[144,896]{1,0:T(8,128)(2,1)S(1)}, bf16[144,896]{1,0:T(8,128)(2,1)S(1)}, u32[]{:S(2)}, u32[]{:S(2)}) collective-permute-start(bf16[144,896]{1,0:T(8,128)(2,1)S(1)} %collective-permute-done.29.refs_20_.refs_52_), channel_id=1, source_target_pairs={{0,8},{8,0},{16,24},{24,16},{1,9},{9,1},{17,25},{25,17},{2,10},{10... | collective-permute-start | bytes 774152 | tf_op jit(solution)/shard_map/ppermute | solution.py:277
  40.0 18.7 %collective-permute-start.33 = (bf16[144,896]{1,0:T(8,128)(2,1)S(1)}, bf16[144,896]{1,0:T(8,128)(2,1)S(1)}, u32[]{:S(2)}, u32[]{:S(2)}) collective-permute-start(bf16[144,896]{1,0:T(8,128)(2,1)S(1)} %collective-permute-done.29.refs_20_.refs_52_), channel_id=1, source_target_pairs={{0,1},{1,0},{2,3},{3,2},{4,5},{5,4},{6,7},{7,6},{8,9},{9,8},{10,11... | collective-permute-start | bytes 774152 | tf_op jit(solution)/shard_map/ppermute | solution.py:277
  42.3 16.4 %collective-permute-start.25 = (bf16[144,896]{1,0:T(8,128)(2,1)S(1)}, bf16[144,896]{1,0:T(8,128)(2,1)S(1)}, u32[]{:S(2)}, u32[]{:S(2)}) collective-permute-start(bf16[144,896]{1,0:T(8,128)(2,1)S(1)} %collective-permute-done.21.refs_12_.refs_44_), channel_id=1, source_target_pairs={{0,1},{1,0},{2,3},{3,2},{4,5},{5,4},{6,7},{7,6},{8,9},{9,8},{10,11... | collective-permute-start | bytes 774152 | tf_op jit(solution)/shard_map/ppermute | solution.py:277
  44.3 16.2 %collective-permute-start.10 = (bf16[144,896]{1,0:T(8,128)(2,1)S(1)}, bf16[144,896]{1,0:T(8,128)(2,1)S(1)}, u32[]{:S(2)}, u32[]{:S(2)}) collective-permute-start(bf16[144,896]{1,0:T(8,128)(2,1)S(1)} %get-tuple-element.32), channel_id=1, source_target_pairs={{0,4},{2,6},{4,0},{6,2},{1,5},{3,7},{5,1},{7,3},{8,12},{10,14},{12... | collective-permute-start | bytes 774152 | tf_op jit(solution)/shard_map/ppermute | solution.py:277
  48.4 17.8 %collective-permute-start.32 = (bf16[144,896]{1,0:T(8,128)(2,1)S(1)}, bf16[144,896]{1,0:T(8,128)(2,1)S(1)}, u32[]{:S(2)}, u32[]{:S(2)}) collective-permute-start(bf16[144,896]{1,0:T(8,128)(2,1)S(1)} %collective-permute-done.9.refs_7_.refs_39_), channel_id=1, source_target_pairs={{0,16},{8,24},{16,0},{24,8},{1,17},{9,25},{17,1},{25,9},{2,18},{10... | collective-permute-start | bytes 774152 | tf_op jit(solution)/shard_map/ppermute | solution.py:277
  54.0 8.0 %copy-start.2 = (bf16[1,512,3584]{2,1,0:T(8,128)(2,1)S(1)}, bf16[1,512,3584]{2,1,0:T(8,128)(2,1)}, u32[]{:S(2)}) copy-start(bf16[1,512,3584]{2,1,0:T(8,128)(2,1)} %w_ref.1) | copy-start | bytes 11010052
  57.9 8.3 %collective-permute-start.24 = (bf16[144,896]{1,0:T(8,128)(2,1)S(1)}, bf16[144,896]{1,0:T(8,128)(2,1)S(1)}, u32[]{:S(2)}, u32[]{:S(2)}) collective-permute-start(bf16[144,896]{1,0:T(8,128)(2,1)S(1)} %collective-permute-done.9.refs_7_.refs_39_), channel_id=1, source_target_pairs={{0,8},{8,0},{16,24},{24,16},{1,9},{9,1},{17,25},{25,17},{2,10},{10... | collective-permute-start | bytes 774152 | tf_op jit(solution)/shard_map/ppermute | solution.py:277
  58.7 8.1 %collective-permute-start.20 = (bf16[144,896]{1,0:T(8,128)(2,1)S(1)}, bf16[144,896]{1,0:T(8,128)(2,1)S(1)}, u32[]{:S(2)}, u32[]{:S(2)}) collective-permute-start(bf16[144,896]{1,0:T(8,128)(2,1)S(1)} %collective-permute-done.9.refs_7_.refs_39_), channel_id=1, source_target_pairs={{0,1},{1,0},{2,3},{3,2},{4,5},{5,4},{6,7},{7,6},{8,9},{9,8},{10,11... | collective-permute-start | bytes 774152 | tf_op jit(solution)/shard_map/ppermute | solution.py:277
  58.7 8.7 %collective-permute-start.34 = (bf16[144,896]{1,0:T(8,128)(2,1)S(1)}, bf16[144,896]{1,0:T(8,128)(2,1)S(1)}, u32[]{:S(2)}, u32[]{:S(2)}) collective-permute-start(bf16[144,896]{1,0:T(8,128)(2,1)S(1)} %collective-permute-done.30.refs_21_.refs_53_), channel_id=1, source_target_pairs={{0,1},{1,0},{2,3},{3,2},{4,5},{5,4},{6,7},{7,6},{8,9},{9,8},{10,11... | collective-permute-start | bytes 774152 | tf_op jit(solution)/shard_map/ppermute | solution.py:277
  60.5 8.4 %collective-permute-start.38 = (bf16[144,896]{1,0:T(8,128)(2,1)S(1)}, bf16[144,896]{1,0:T(8,128)(2,1)S(1)}, u32[]{:S(2)}, u32[]{:S(2)}) collective-permute-start(bf16[144,896]{1,0:T(8,128)(2,1)S(1)} %collective-permute-done.22.refs_13_.refs_45_), channel_id=1, source_target_pairs={{0,16},{8,24},{16,0},{24,8},{1,17},{9,25},{17,1},{25,9},{2,18},{10... | collective-permute-start | bytes 774152 | tf_op jit(solution)/shard_map/ppermute | solution.py:277
  66.2 31.5 %collective-permute-start.7 = (bf16[4,144,896]{2,1,0:T(8,128)(2,1)S(1)}, bf16[4,144,896]{2,1,0:T(8,128)(2,1)S(1)}, u32[]{:S(2)}, u32[]{:S(2)}) collective-permute-start(bf16[4,144,896]{2,1,0:T(8,128)(2,1)S(1)} %get-tuple-element.25), channel_id=1, source_target_pairs={{0,1},{1,0},{2,3},{3,2},{4,5},{5,4},{6,7},{7,6},{8,9},{9,8},{10,11... | collective-permute-start | bytes 3096584 | tf_op jit(solution)/shard_map/ppermute | solution.py:277
  66.3 3.0 %collective-permute-start.26 = (bf16[144,896]{1,0:T(8,128)(2,1)S(1)}, bf16[144,896]{1,0:T(8,128)(2,1)S(1)}, u32[]{:S(2)}, u32[]{:S(2)}) collective-permute-start(bf16[144,896]{1,0:T(8,128)(2,1)S(1)} %collective-permute-done.22.refs_13_.refs_45_), channel_id=1, source_target_pairs={{0,1},{1,0},{2,3},{3,2},{4,5},{5,4},{6,7},{7,6},{8,9},{9,8},{10,11... | collective-permute-start | bytes 774152 | tf_op jit(solution)/shard_map/ppermute | solution.py:277
  66.8 10.8 %collective-permute-start.15 = (bf16[288,512]{1,0:T(8,128)(2,1)S(1)}, bf16[288,512]{1,0:T(8,128)(2,1)S(1)}, u32[]{:S(2)}, u32[]{:S(2)}) collective-permute-start(bf16[288,512]{1,0:T(8,128)(2,1)S(1)} %shard_map.87.hidden_ref.refs_0_), channel_id=1, source_target_pairs={{0,24},{8,16},{16,8},{24,0},{1,25},{9,17},{17,9},{25,1},{2,26},{10... | collective-permute-start | bytes 884744 | tf_op jit(solution)/shard_map/ppermute | solution.py:277
  67.4 15.7 %collective-permute-start.14 = (bf16[288,512]{1,0:T(8,128)(2,1)S(1)}, bf16[288,512]{1,0:T(8,128)(2,1)S(1)}, u32[]{:S(2)}, u32[]{:S(2)}) collective-permute-start(bf16[288,512]{1,0:T(8,128)(2,1)S(1)} %shard_map.87.hidden_ref.refs_0_), channel_id=1, source_target_pairs={{0,16},{8,24},{16,0},{24,8},{1,17},{9,25},{17,1},{25,9},{2,18},{10... | collective-permute-start | bytes 884744 | tf_op jit(solution)/shard_map/ppermute | solution.py:277
  68.9 1.5 %collective-permute-start.41 = (bf16[144,896]{1,0:T(8,128)(2,1)S(1)}, bf16[144,896]{1,0:T(8,128)(2,1)S(1)}, u32[]{:S(2)}, u32[]{:S(2)}) collective-permute-start(bf16[144,896]{1,0:T(8,128)(2,1)S(1)} %collective-permute-done.37.refs_28_.refs_60_), channel_id=1, source_target_pairs={{0,1},{1,0},{2,3},{3,2},{4,5},{5,4},{6,7},{7,6},{8,9},{9,8},{10,11... | collective-permute-start | bytes 774152 | tf_op jit(solution)/shard_map/ppermute | solution.py:277
  69.3 13.9 %collective-permute-start.13 = (bf16[288,512]{1,0:T(8,128)(2,1)S(1)}, bf16[288,512]{1,0:T(8,128)(2,1)S(1)}, u32[]{:S(2)}, u32[]{:S(2)}) collective-permute-start(bf16[288,512]{1,0:T(8,128)(2,1)S(1)} %shard_map.87.hidden_ref.refs_0_), channel_id=1, source_target_pairs={{0,8},{8,0},{16,24},{24,16},{1,9},{9,1},{17,25},{25,17},{2,10},{10... | collective-permute-start | bytes 884744 | tf_op jit(solution)/shard_map/ppermute | solution.py:277
  70.4 17.5 %collective-permute-start.31 = (bf16[144,896]{1,0:T(8,128)(2,1)S(1)}, bf16[144,896]{1,0:T(8,128)(2,1)S(1)}, u32[]{:S(2)}, u32[]{:S(2)}) collective-permute-start(bf16[144,896]{1,0:T(8,128)(2,1)S(1)} %collective-permute-done.10.refs_6_.refs_38_), channel_id=1, source_target_pairs={{0,16},{8,24},{16,0},{24,8},{1,17},{9,25},{17,1},{25,9},{2,18},{10... | collective-permute-start | bytes 774152 | tf_op jit(solution)/shard_map/ppermute | solution.py:277
  77.6 11.4 %collective-permute-start.23 = (bf16[144,896]{1,0:T(8,128)(2,1)S(1)}, bf16[144,896]{1,0:T(8,128)(2,1)S(1)}, u32[]{:S(2)}, u32[]{:S(2)}) collective-permute-start(bf16[144,896]{1,0:T(8,128)(2,1)S(1)} %collective-permute-done.10.refs_6_.refs_38_), channel_id=1, source_target_pairs={{0,8},{8,0},{16,24},{24,16},{1,9},{9,1},{17,25},{25,17},{2,10},{10... | collective-permute-start | bytes 774152 | tf_op jit(solution)/shard_map/ppermute | solution.py:277
  83.1 5.9 %collective-permute-start.19 = (bf16[144,896]{1,0:T(8,128)(2,1)S(1)}, bf16[144,896]{1,0:T(8,128)(2,1)S(1)}, u32[]{:S(2)}, u32[]{:S(2)}) collective-permute-start(bf16[144,896]{1,0:T(8,128)(2,1)S(1)} %collective-permute-done.10.refs_6_.refs_38_), channel_id=1, source_target_pairs={{0,1},{1,0},{2,3},{3,2},{4,5},{5,4},{6,7},{7,6},{8,9},{9,8},{10,11... | collective-permute-start | bytes 774152 | tf_op jit(solution)/shard_map/ppermute | solution.py:277
  83.1 6.7 %collective-permute-start.36 = (bf16[144,896]{1,0:T(8,128)(2,1)S(1)}, bf16[144,896]{1,0:T(8,128)(2,1)S(1)}, u32[]{:S(2)}, u32[]{:S(2)}) collective-permute-start(bf16[144,896]{1,0:T(8,128)(2,1)S(1)} %collective-permute-done.32.refs_23_.refs_55_), channel_id=1, source_target_pairs={{0,1},{1,0},{2,3},{3,2},{4,5},{5,4},{6,7},{7,6},{8,9},{9,8},{10,11... | collective-permute-start | bytes 774152 | tf_op jit(solution)/shard_map/ppermute | solution.py:277
  88.0 7.6 %collective-permute-start.40 = (bf16[144,896]{1,0:T(8,128)(2,1)S(1)}, bf16[144,896]{1,0:T(8,128)(2,1)S(1)}, u32[]{:S(2)}, u32[]{:S(2)}) collective-permute-start(bf16[144,896]{1,0:T(8,128)(2,1)S(1)} %collective-permute-done.24.refs_15_.refs_47_), channel_id=1, source_target_pairs={{0,16},{8,24},{16,0},{24,8},{1,17},{9,25},{17,1},{25,9},{2,18},{10... | collective-permute-start | bytes 774152 | tf_op jit(solution)/shard_map/ppermute | solution.py:277
  89.0 6.5 %collective-permute-start.28 = (bf16[144,896]{1,0:T(8,128)(2,1)S(1)}, bf16[144,896]{1,0:T(8,128)(2,1)S(1)}, u32[]{:S(2)}, u32[]{:S(2)}) collective-permute-start(bf16[144,896]{1,0:T(8,128)(2,1)S(1)} %collective-permute-done.24.refs_15_.refs_47_), channel_id=1, source_target_pairs={{0,1},{1,0},{2,3},{3,2},{4,5},{5,4},{6,7},{7,6},{8,9},{9,8},{10,11... | collective-permute-start | bytes 774152 | tf_op jit(solution)/shard_map/ppermute | solution.py:277
  89.0 8.6 %collective-permute-start.39 = (bf16[144,896]{1,0:T(8,128)(2,1)S(1)}, bf16[144,896]{1,0:T(8,128)(2,1)S(1)}, u32[]{:S(2)}, u32[]{:S(2)}) collective-permute-start(bf16[144,896]{1,0:T(8,128)(2,1)S(1)} %collective-permute-done.31.refs_22_.refs_54_), channel_id=1, source_target_pairs={{0,8},{8,0},{16,24},{24,16},{1,9},{9,1},{17,25},{25,17},{2,10},{10... | collective-permute-start | bytes 774152 | tf_op jit(solution)/shard_map/ppermute | solution.py:277
  89.8 8.6 %collective-permute-start.42 = (bf16[144,896]{1,0:T(8,128)(2,1)S(1)}, bf16[144,896]{1,0:T(8,128)(2,1)S(1)}, u32[]{:S(2)}, u32[]{:S(2)}) collective-permute-start(bf16[144,896]{1,0:T(8,128)(2,1)S(1)} %collective-permute-done.38.refs_29_.refs_61_), channel_id=1, source_target_pairs={{0,1},{1,0},{2,3},{3,2},{4,5},{5,4},{6,7},{7,6},{8,9},{9,8},{10,11... | collective-permute-start | bytes 774152 | tf_op jit(solution)/shard_map/ppermute | solution.py:277
  95.5 3.5 %collective-permute-start.35 = (bf16[144,896]{1,0:T(8,128)(2,1)S(1)}, bf16[144,896]{1,0:T(8,128)(2,1)S(1)}, u32[]{:S(2)}, u32[]{:S(2)}) collective-permute-start(bf16[144,896]{1,0:T(8,128)(2,1)S(1)} %collective-permute-done.31.refs_22_.refs_54_), channel_id=1, source_target_pairs={{0,1},{1,0},{2,3},{3,2},{4,5},{5,4},{6,7},{7,6},{8,9},{9,8},{10,11... | collective-permute-start | bytes 774152 | tf_op jit(solution)/shard_map/ppermute | solution.py:277
  95.5 3.5 %collective-permute-start.27 = (bf16[144,896]{1,0:T(8,128)(2,1)S(1)}, bf16[144,896]{1,0:T(8,128)(2,1)S(1)}, u32[]{:S(2)}, u32[]{:S(2)}) collective-permute-start(bf16[144,896]{1,0:T(8,128)(2,1)S(1)} %collective-permute-done.23.refs_14_.refs_46_), channel_id=1, source_target_pairs={{0,1},{1,0},{2,3},{3,2},{4,5},{5,4},{6,7},{7,6},{8,9},{9,8},{10,11... | collective-permute-start | bytes 774152 | tf_op jit(solution)/shard_map/ppermute | solution.py:277
  97.7 5.2 %collective-permute-start.44 = (bf16[144,896]{1,0:T(8,128)(2,1)S(1)}, bf16[144,896]{1,0:T(8,128)(2,1)S(1)}, u32[]{:S(2)}, u32[]{:S(2)}) collective-permute-start(bf16[144,896]{1,0:T(8,128)(2,1)S(1)} %collective-permute-done.40.refs_31_.refs_63_), channel_id=1, source_target_pairs={{0,1},{1,0},{2,3},{3,2},{4,5},{5,4},{6,7},{7,6},{8,9},{9,8},{10,11... | collective-permute-start | bytes 774152 | tf_op jit(solution)/shard_map/ppermute | solution.py:277
  97.7 5.2 %collective-permute-start.43 = (bf16[144,896]{1,0:T(8,128)(2,1)S(1)}, bf16[144,896]{1,0:T(8,128)(2,1)S(1)}, u32[]{:S(2)}, u32[]{:S(2)}) collective-permute-start(bf16[144,896]{1,0:T(8,128)(2,1)S(1)} %collective-permute-done.39.refs_30_.refs_62_), channel_id=1, source_target_pairs={{0,1},{1,0},{2,3},{3,2},{4,5},{5,4},{6,7},{7,6},{8,9},{9,8},{10,11... | collective-permute-start | bytes 774152 | tf_op jit(solution)/shard_map/ppermute | solution.py:277
  98.4 12.4 %collective-permute-start.12 = (bf16[144,896]{1,0:T(8,128)(2,1)S(1)}, bf16[144,896]{1,0:T(8,128)(2,1)S(1)}, u32[]{:S(2)}, u32[]{:S(2)}) collective-permute-start(bf16[144,896]{1,0:T(8,128)(2,1)S(1)} %get-tuple-element.35), channel_id=1, source_target_pairs={{0,6},{2,4},{4,2},{6,0},{1,7},{3,5},{5,3},{7,1},{8,14},{10,12},{12... | collective-permute-start | bytes 774152 | tf_op jit(solution)/shard_map/ppermute | solution.py:277
  99.0 22.2 %collective-permute-start.11 = (bf16[144,896]{1,0:T(8,128)(2,1)S(1)}, bf16[144,896]{1,0:T(8,128)(2,1)S(1)}, u32[]{:S(2)}, u32[]{:S(2)}) collective-permute-start(bf16[144,896]{1,0:T(8,128)(2,1)S(1)} %get-tuple-element.33), channel_id=1, source_target_pairs={{0,4},{2,6},{4,0},{6,2},{1,5},{3,7},{5,1},{7,3},{8,12},{10,14},{12... | collective-permute-start | bytes 774152 | tf_op jit(solution)/shard_map/ppermute | solution.py:277
  99.0 22.2 %copy-start.6 = (s32[128,1]{0,1:T(1,128)S(1)}, s32[128,1]{0,1:T(1,128)}, u32[]{:S(2)}) copy-start(s32[128,1]{0,1:T(1,128)} %param.9) | copy-start | bytes 1540
  99.1 22.2 %copy-start.8 = (f32[128,1]{0,1:T(1,128)S(1)}, f32[128,1]{0,1:T(1,128)}, u32[]{:S(2)}) copy-start(f32[128,1]{0,1:T(1,128)} %param.10) | copy-start | bytes 1540
  99.1 22.2 %collective-permute-start.8 = (bf16[144,896]{1,0:T(8,128)(2,1)S(1)}, bf16[144,896]{1,0:T(8,128)(2,1)S(1)}, u32[]{:S(2)}, u32[]{:S(2)}) collective-permute-start(bf16[144,896]{1,0:T(8,128)(2,1)S(1)} %get-tuple-element.27), channel_id=1, source_target_pairs={{0,2},{2,0},{4,6},{6,4},{1,3},{3,1},{5,7},{7,5},{8,10},{10,8},{12,... | collective-permute-start | bytes 774152 | tf_op jit(solution)/shard_map/ppermute | solution.py:277
  (6 other events, 7.7 us)

commit v3 on v2

--- a/solution.py
+++ b/solution.py
@@ -137,7 +137,7 @@
         out_specs=pl.BlockSpec((total, fh), lambda q: (0, 0)),
         out_shape=jax.ShapeDtypeStruct((total, fh), BF),
         scratch_shapes=[pltpu.VMEM((total, fh), F32)] * 2,
-        compiler_params=PARAMS,
+        compiler_params=pltpu.CompilerParams(vmem_limit_bytes=50 * 1024 * 1024),
         cost_estimate=pl.CostEstimate(flops=4 * total * fh * piece * QUARTERS, bytes_accessed=4 * fh * piece * QUARTERS, transcendentals=total * fh),
     )(*folded, w_gate, w_up)
 

time: 123 us -> 123 us (level)
  local copies, waits for them, and re-layouts: 7.75 us -> 3.67 us
  Pallas kernels: 19.2 us -> 21.3 us
  waiting for transfers between devices: 55.5 us -> 57.2 us
    unnamed x18 -> x14, local copies, waits for them, and re-layouts: 7.75 us -> 3.67 us
    pallas_call x1, Pallas kernels: 3.93 us -> 6.06 us  [hidden_of(): pl.pallas_call(functools.partial(hidden_kernel, main, rem), grid=(QUARTER...]
    ppermute x45, waiting for transfers between devices: 55.5 us -> 57.2 us  [by_xor(): lax.ppermute(x, axis, [(i, i ^ k) for i in range(lax.axis_size(axis))])]
  transfers between devices with their start and end apart: 45 -> 45, of which waited for: 15 -> 15; matrix products, arithmetic and copies ran while one was open for 0% -> 0% of each run, Pallas kernels for 14% -> 16%
where the time goes in v3:
time: 123 us
  waiting for transfers between devices  57.2 us (47%)
  starting transfers between devices  39.7 us (32%)
  Pallas kernels  21.3 us (17%)
  local copies, waits for them, and re-layouts  3.67 us (3%)
    ppermute x45, waiting for transfers between devices, by_xor(): lax.ppermute(x, axis, [(i, i ^ k) for i in range(lax.axis_size(axis))])  57.2 us
    ppermute x45, starting transfers between devices, by_xor(): lax.ppermute(x, axis, [(i, i ^ k) for i in range(lax.axis_size(axis))])  39.7 us
    pallas_call x1, Pallas kernels, gradient(): pl.pallas_call(functools.partial(grad_kernel, main, rem, capacity, groups...  7.9 us
    pallas_call x1, Pallas kernels, hidden_of(): pl.pallas_call(functools.partial(hidden_kernel, main, rem), grid=(QUARTER...  6.06 us
    pallas_call x1, Pallas kernels, down_of(): pl.pallas_call(functools.partial(down_kernel, main, rem, capacity), grid=...  4.15 us
    unnamed x14, local copies, waits for them, and re-layouts  3.67 us
  transfers between devices with their start and end apart: 45, of which 15 were waited for; matrix products, arithmetic and copies ran while one was open for 0% of the time, Pallas kernels for 16%

profile of v3, /device:TPU:0, one launch (start us, length us, event | category | flops | bytes accessed | tf_op | source)
XLA Modules:
  0.0 122.6 jit_solution(3694114830440799327)
XLA Ops:
  0.6 1.2 copy-done.1
  1.8 0.7 copy-done.3
  2.5 0.7 shard_map.86
  3.1 3.1 %collective-permute-start = (bf16[144,896]{1,0:T(8,128)(2,1)S(1)}, bf16[144,896]{1,0:T(8,128)(2,1)S(1)}, u32[]{:S(2)}, u32[]{:S(2)}) collective-permute-start(bf16[144,896]{1,0:T(8,128)(2,1)S(1)} %get-tuple-element.21), channel_id=1, source_target_pairs={{0,2},{2,0},{4,6},{6,4},{1,3},{3,1},{5,7},{7,5},{8,10},{10,8},{12,... | collective-permute-start | bytes 774152 | tf_op jit(solution)/shard_map/ppermute | solution.py:277
  6.2 2.6 %collective-permute-start.1 = (bf16[144,896]{1,0:T(8,128)(2,1)S(1)}, bf16[144,896]{1,0:T(8,128)(2,1)S(1)}, u32[]{:S(2)}, u32[]{:S(2)}) collective-permute-start(bf16[144,896]{1,0:T(8,128)(2,1)S(1)} %get-tuple-element.22), channel_id=1, source_target_pairs={{0,4},{2,6},{4,0},{6,2},{1,5},{3,7},{5,1},{7,3},{8,12},{10,14},{12... | collective-permute-start | bytes 774152 | tf_op jit(solution)/shard_map/ppermute | solution.py:277
  8.8 1.2 copy-done.2
  10.0 0.7 copy-done.5
  10.7 0.7 shard_map.90
  11.4 0.9 collective-permute-start.16
  12.3 5.7 %collective-permute-done.refs_1_ = bf16[144,896]{1,0:T(8,128)(2,1)S(1)} collective-permute-done((bf16[144,896]{1,0:T(8,128)(2,1)S(1)}, bf16[144,896]{1,0:T(8,128)(2,1)S(1)}, u32[]{:S(2)}, u32[]{:S(2)}) %collective-permute-start) | collective-permute-done | bytes 258080 | tf_op jit(solution)/shard_map/ppermute | solution.py:277
  18.0 2.0 %collective-permute-start.29 = (bf16[144,896]{1,0:T(8,128)(2,1)S(1)}, bf16[144,896]{1,0:T(8,128)(2,1)S(1)}, u32[]{:S(2)}, u32[]{:S(2)}) collective-permute-start(bf16[144,896]{1,0:T(8,128)(2,1)S(1)} %get-tuple-element.36.refs_4_.refs_36_), channel_id=1, source_target_pairs={{0,16},{8,24},{16,0},{24,8},{1,17},{9,25},{17,1},{25,9},{2,18},{10... | collective-permute-start | bytes 774152 | tf_op jit(solution)/shard_map/ppermute | solution.py:277
  20.0 7.3 %collective-permute-done.1.refs_2_ = bf16[144,896]{1,0:T(8,128)(2,1)S(1)} collective-permute-done((bf16[144,896]{1,0:T(8,128)(2,1)S(1)}, bf16[144,896]{1,0:T(8,128)(2,1)S(1)}, u32[]{:S(2)}, u32[]{:S(2)}) %collective-permute-start.1) | collective-permute-done | bytes 258080 | tf_op jit(solution)/shard_map/ppermute | solution.py:277
  27.4 1.5 %collective-permute-start.21 = (bf16[144,896]{1,0:T(8,128)(2,1)S(1)}, bf16[144,896]{1,0:T(8,128)(2,1)S(1)}, u32[]{:S(2)}, u32[]{:S(2)}) collective-permute-start(bf16[144,896]{1,0:T(8,128)(2,1)S(1)} %get-tuple-element.36.refs_4_.refs_36_), channel_id=1, source_target_pairs={{0,8},{8,0},{16,24},{24,16},{1,9},{9,1},{17,25},{25,17},{2,10},{10... | collective-permute-start | bytes 774152 | tf_op jit(solution)/shard_map/ppermute | solution.py:277
  29.4 3.4 %collective-permute-start.9 = (bf16[144,896]{1,0:T(8,128)(2,1)S(1)}, bf16[144,896]{1,0:T(8,128)(2,1)S(1)}, u32[]{:S(2)}, u32[]{:S(2)}) collective-permute-start(bf16[144,896]{1,0:T(8,128)(2,1)S(1)} %get-tuple-element.31), channel_id=1, source_target_pairs={{0,6},{2,4},{4,2},{6,0},{1,7},{3,5},{5,3},{7,1},{8,14},{10,12},{12... | collective-permute-start | bytes 774152 | tf_op jit(solution)/shard_map/ppermute | solution.py:277
  32.8 0.9 collective-permute-done.21.refs_12_.refs_44_
  33.7 1.5 %collective-permute-start.30 = (bf16[144,896]{1,0:T(8,128)(2,1)S(1)}, bf16[144,896]{1,0:T(8,128)(2,1)S(1)}, u32[]{:S(2)}, u32[]{:S(2)}) collective-permute-start(bf16[144,896]{1,0:T(8,128)(2,1)S(1)} %collective-permute-done.16.refs_5_.refs_37_), channel_id=1, source_target_pairs={{0,16},{8,24},{16,0},{24,8},{1,17},{9,25},{17,1},{25,9},{2,18},{10... | collective-permute-start | bytes 774152 | tf_op jit(solution)/shard_map/ppermute | solution.py:277
  35.2 1.5 %collective-permute-start.22 = (bf16[144,896]{1,0:T(8,128)(2,1)S(1)}, bf16[144,896]{1,0:T(8,128)(2,1)S(1)}, u32[]{:S(2)}, u32[]{:S(2)}) collective-permute-start(bf16[144,896]{1,0:T(8,128)(2,1)S(1)} %collective-permute-done.16.refs_5_.refs_37_), channel_id=1, source_target_pairs={{0,8},{8,0},{16,24},{24,16},{1,9},{9,1},{17,25},{25,17},{2,10},{10... | collective-permute-start | bytes 774152 | tf_op jit(solution)/shard_map/ppermute | solution.py:277
  36.7 2.8 %collective-permute-done.9.refs_7_.refs_39_ = bf16[144,896]{1,0:T(8,128)(2,1)S(1)} collective-permute-done((bf16[144,896]{1,0:T(8,128)(2,1)S(1)}, bf16[144,896]{1,0:T(8,128)(2,1)S(1)}, u32[]{:S(2)}, u32[]{:S(2)}) %collective-permute-start.9) | collective-permute-done | bytes 258080 | tf_op jit(solution)/shard_map/ppermute | solution.py:277
  39.5 0.6 collective-permute-start.37
  40.2 2.1 %collective-permute-done.30.refs_21_.refs_53_ = bf16[144,896]{1,0:T(8,128)(2,1)S(1)} collective-permute-done((bf16[144,896]{1,0:T(8,128)(2,1)S(1)}, bf16[144,896]{1,0:T(8,128)(2,1)S(1)}, u32[]{:S(2)}, u32[]{:S(2)}) %collective-permute-start.30) | collective-permute-done | bytes 258080 | tf_op jit(solution)/shard_map/ppermute | solution.py:277
  42.3 2.0 %collective-permute-done.22.refs_13_.refs_45_ = bf16[144,896]{1,0:T(8,128)(2,1)S(1)} collective-permute-done((bf16[144,896]{1,0:T(8,128)(2,1)S(1)}, bf16[144,896]{1,0:T(8,128)(2,1)S(1)}, u32[]{:S(2)}, u32[]{:S(2)}) %collective-permute-start.22) | collective-permute-done | bytes 258080 | tf_op jit(solution)/shard_map/ppermute | solution.py:277
  44.3 4.1 %collective-permute-start.10 = (bf16[144,896]{1,0:T(8,128)(2,1)S(1)}, bf16[144,896]{1,0:T(8,128)(2,1)S(1)}, u32[]{:S(2)}, u32[]{:S(2)}) collective-permute-start(bf16[144,896]{1,0:T(8,128)(2,1)S(1)} %get-tuple-element.32), channel_id=1, source_target_pairs={{0,4},{2,6},{4,0},{6,2},{1,5},{3,7},{5,1},{7,3},{8,12},{10,14},{12... | collective-permute-start | bytes 774152 | tf_op jit(solution)/shard_map/ppermute | solution.py:277
  48.4 1.5 %collective-permute-start.32 = (bf16[144,896]{1,0:T(8,128)(2,1)S(1)}, bf16[144,896]{1,0:T(8,128)(2,1)S(1)}, u32[]{:S(2)}, u32[]{:S(2)}) collective-permute-start(bf16[144,896]{1,0:T(8,128)(2,1)S(1)} %collective-permute-done.9.refs_7_.refs_39_), channel_id=1, source_target_pairs={{0,16},{8,24},{16,0},{24,8},{1,17},{9,25},{17,1},{25,9},{2,18},{10... | collective-permute-start | bytes 774152 | tf_op jit(solution)/shard_map/ppermute | solution.py:277
  49.9 6.1 %shard_map.87.hidden_ref.refs_0_ = bf16[288,512]{1,0:T(8,128)(2,1)S(1)} custom-call(bf16[144,896]{1,0:T(8,128)(2,1)S(1)} %get-tuple-element.20.refs_0_, bf16[144,896]{1,0:T(8,128)(2,1)S(1)} %collective-permute-done.refs_1_, bf16[144,896]{1,0:T(8,128)(2,1)S(1)} %collective-permute-done.1.refs_2_, bf16[144,896]{1,0:T(8,128)(2,1)S(1)} %collective-permute-done.2.refs_3_, ...), custom_call_target="tpu_custom_call" | custom-call | flops 2113929216 | bytes 7340032 | tf_op jit(solution)/shard_map/pallas_call | solution.py:133
  56.0 0.7 collective-permute-start.24
  57.3 3.2 %collective-permute-done.10.refs_6_.refs_38_ = bf16[144,896]{1,0:T(8,128)(2,1)S(1)} collective-permute-done((bf16[144,896]{1,0:T(8,128)(2,1)S(1)}, bf16[144,896]{1,0:T(8,128)(2,1)S(1)}, u32[]{:S(2)}, u32[]{:S(2)}) %collective-permute-start.10) | collective-permute-done | bytes 258080 | tf_op jit(solution)/shard_map/ppermute | solution.py:277
  60.5 1.5 %collective-permute-start.38 = (bf16[144,896]{1,0:T(8,128)(2,1)S(1)}, bf16[144,896]{1,0:T(8,128)(2,1)S(1)}, u32[]{:S(2)}, u32[]{:S(2)}) collective-permute-start(bf16[144,896]{1,0:T(8,128)(2,1)S(1)} %collective-permute-done.22.refs_13_.refs_45_), channel_id=1, source_target_pairs={{0,16},{8,24},{16,0},{24,8},{1,17},{9,25},{17,1},{25,9},{2,18},{10... | collective-permute-start | bytes 774152 | tf_op jit(solution)/shard_map/ppermute | solution.py:277
  62.0 4.1 %shard_map.88 = (bf16[4,144,896]{2,1,0:T(8,128)(2,1)S(1)}, bf16[4,144,896]{2,1,0:T(8,128)(2,1)S(1)}) custom-call(bf16[288,512]{1,0:T(8,128)(2,1)S(1)} %shard_map.87.hidden_ref.refs_0_, bf16[1,512,3584]{2,1,0:T(8,128)(2,1)S(1)} %copy-done), custom_call_target="tpu_custom_call" | custom-call | flops 1056964608 | bytes 3670016 | tf_op jit(solution)/shard_map/pallas_call | solution.py:176
  66.8 0.6 collective-permute-start.15
  67.4 1.5 %collective-permute-start.14 = (bf16[288,512]{1,0:T(8,128)(2,1)S(1)}, bf16[288,512]{1,0:T(8,128)(2,1)S(1)}, u32[]{:S(2)}, u32[]{:S(2)}) collective-permute-start(bf16[288,512]{1,0:T(8,128)(2,1)S(1)} %shard_map.87.hidden_ref.refs_0_), channel_id=1, source_target_pairs={{0,16},{8,24},{16,0},{24,8},{1,17},{9,25},{17,1},{25,9},{2,18},{10... | collective-permute-start | bytes 884744 | tf_op jit(solution)/shard_map/ppermute | solution.py:277
  69.3 1.1 collective-permute-start.13
  70.4 1.0 collective-permute-start.31
  71.5 6.1 %collective-permute-done.15.refs_3_ = bf16[288,512]{1,0:T(8,128)(2,1)S(1)} collective-permute-done((bf16[288,512]{1,0:T(8,128)(2,1)S(1)}, bf16[288,512]{1,0:T(8,128)(2,1)S(1)}, u32[]{:S(2)}, u32[]{:S(2)}) %collective-permute-start.15) | collective-permute-done | bytes 294944 | tf_op jit(solution)/shard_map/ppermute | solution.py:277
  77.6 0.7 collective-permute-start.23
  78.3 4.8 %collective-permute-done.14.refs_2_ = bf16[288,512]{1,0:T(8,128)(2,1)S(1)} collective-permute-done((bf16[288,512]{1,0:T(8,128)(2,1)S(1)}, bf16[288,512]{1,0:T(8,128)(2,1)S(1)}, u32[]{:S(2)}, u32[]{:S(2)}) %collective-permute-start.14) | collective-permute-done | bytes 294944 | tf_op jit(solution)/shard_map/ppermute | solution.py:277
  83.1 0.5 collective-permute-start.36
  83.6 4.3 %collective-permute-done.31.refs_22_.refs_54_ = bf16[144,896]{1,0:T(8,128)(2,1)S(1)} collective-permute-done((bf16[144,896]{1,0:T(8,128)(2,1)S(1)}, bf16[144,896]{1,0:T(8,128)(2,1)S(1)}, u32[]{:S(2)}, u32[]{:S(2)}) %collective-permute-start.31) | collective-permute-done | bytes 258080 | tf_op jit(solution)/shard_map/ppermute | solution.py:277
  88.0 1.1 collective-permute-start.40
  89.1 0.7 collective-permute-start.39
  89.9 5.6 %collective-permute-done.40.refs_31_.refs_63_ = bf16[144,896]{1,0:T(8,128)(2,1)S(1)} collective-permute-done((bf16[144,896]{1,0:T(8,128)(2,1)S(1)}, bf16[144,896]{1,0:T(8,128)(2,1)S(1)}, u32[]{:S(2)}, u32[]{:S(2)}) %collective-permute-start.40) | collective-permute-done | bytes 258080 | tf_op jit(solution)/shard_map/ppermute | solution.py:277
  95.5 0.5 collective-permute-start.27
  96.0 1.6 %collective-permute-done.39.refs_30_.refs_62_ = bf16[144,896]{1,0:T(8,128)(2,1)S(1)} collective-permute-done((bf16[144,896]{1,0:T(8,128)(2,1)S(1)}, bf16[144,896]{1,0:T(8,128)(2,1)S(1)}, u32[]{:S(2)}, u32[]{:S(2)}) %collective-permute-start.39) | collective-permute-done | bytes 258080 | tf_op jit(solution)/shard_map/ppermute | solution.py:277
  97.7 0.5 collective-permute-start.43
  98.5 0.6 collective-permute-start.12
  99.1 3.9 %collective-permute-start.8 = (bf16[144,896]{1,0:T(8,128)(2,1)S(1)}, bf16[144,896]{1,0:T(8,128)(2,1)S(1)}, u32[]{:S(2)}, u32[]{:S(2)}) collective-permute-start(bf16[144,896]{1,0:T(8,128)(2,1)S(1)} %get-tuple-element.27), channel_id=1, source_target_pairs={{0,2},{2,0},{4,6},{6,4},{1,3},{3,1},{5,7},{7,5},{8,10},{10,8},{12,... | collective-permute-start | bytes 774152 | tf_op jit(solution)/shard_map/ppermute | solution.py:277
  102.9 7.9 %shard_map.92 = bf16[1,512,3584]{2,1,0:T(8,128)(2,1)} custom-call(bf16[288,512]{1,0:T(8,128)(2,1)S(1)} %shard_map.87.hidden_ref.refs_0_, bf16[288,512]{1,0:T(8,128)(2,1)S(1)} %collective-permute-done.13.refs_1_, bf16[288,512]{1,0:T(8,128)(2,1)S(1)} %collective-permute-done.14.refs_2_, bf16[288,512]{1,0:T(8,128)(2,1)S(1)} %collective-permute-done.15.refs_3_, ...), custom_call_target="tpu_custom_call" | custom-call | flops 4227858432 | bytes 11927552 | tf_op jit(solution)/shard_map/pallas_call | solution.py:263
  110.8 10.2 %collective-permute-done.11.refs_2_ = bf16[144,896]{1,0:T(8,128)(2,1)S(1)} collective-permute-done((bf16[144,896]{1,0:T(8,128)(2,1)S(1)}, bf16[144,896]{1,0:T(8,128)(2,1)S(1)}, u32[]{:S(2)}, u32[]{:S(2)}) %collective-permute-start.11) | collective-permute-done | bytes 258080 | tf_op jit(solution)/shard_map/ppermute | solution.py:277
  121.0 1.6 %shard_map.91 = bf16[128,3584]{1,0:T(8,128)(2,1)} custom-call(s32[1,128]{1,0:T(1,128)S(1)} %bitcast.4, f32[1,128]{1,0:T(1,128)S(1)} %bitcast.6, bf16[144,896]{1,0:T(8,128)(2,1)S(1)} %get-tuple-element.26.refs_0_, bf16[144,896]{1,0:T(8,128)(2,1)S(1)} %collective-permute-done.8.refs_1_, bf16[144,896]{1,0:T(8,128)(2,1)S(1)} %collective-permute-done.11.refs_2_, ...), custom_call_target="tpu_custom_call" | custom-call | flops 117440512 | bytes 1835008 | tf_op jit(solution)/shard_map/pallas_call | solution.py:221
  (63 shorter events, 2.7 us)
Async XLA Ops:
  3.1 14.9 %collective-permute-start = (bf16[144,896]{1,0:T(8,128)(2,1)S(1)}, bf16[144,896]{1,0:T(8,128)(2,1)S(1)}, u32[]{:S(2)}, u32[]{:S(2)}) collective-permute-start(bf16[144,896]{1,0:T(8,128)(2,1)S(1)} %get-tuple-element.21), channel_id=1, source_target_pairs={{0,2},{2,0},{4,6},{6,4},{1,3},{3,1},{5,7},{7,5},{8,10},{10,8},{12,... | collective-permute-start | bytes 774152 | tf_op jit(solution)/shard_map/ppermute | solution.py:277
  6.2 21.1 %collective-permute-start.1 = (bf16[144,896]{1,0:T(8,128)(2,1)S(1)}, bf16[144,896]{1,0:T(8,128)(2,1)S(1)}, u32[]{:S(2)}, u32[]{:S(2)}) collective-permute-start(bf16[144,896]{1,0:T(8,128)(2,1)S(1)} %get-tuple-element.22), channel_id=1, source_target_pairs={{0,4},{2,6},{4,0},{6,2},{1,5},{3,7},{5,1},{7,3},{8,12},{10,14},{12... | collective-permute-start | bytes 774152 | tf_op jit(solution)/shard_map/ppermute | solution.py:277
  8.8 20.0 %collective-permute-start.2 = (bf16[144,896]{1,0:T(8,128)(2,1)S(1)}, bf16[144,896]{1,0:T(8,128)(2,1)S(1)}, u32[]{:S(2)}, u32[]{:S(2)}) collective-permute-start(bf16[144,896]{1,0:T(8,128)(2,1)S(1)} %get-tuple-element.23), channel_id=1, source_target_pairs={{0,6},{2,4},{4,2},{6,0},{1,7},{3,5},{5,3},{7,1},{8,14},{10,12},{12... | collective-permute-start | bytes 774152 | tf_op jit(solution)/shard_map/ppermute | solution.py:277
  8.8 20.1 %collective-permute-start.3 = (bf16[144,896]{1,0:T(8,128)(2,1)S(1)}, bf16[144,896]{1,0:T(8,128)(2,1)S(1)}, u32[]{:S(2)}, u32[]{:S(2)}) collective-permute-start(bf16[144,896]{1,0:T(8,128)(2,1)S(1)} %get-tuple-element.20.refs_0_), channel_id=1, source_target_pairs={{0,1},{1,0},{2,3},{3,2},{4,5},{5,4},{6,7},{7,6},{8,9},{9,8},{10,11... | collective-permute-start | bytes 774152 | tf_op jit(solution)/shard_map/ppermute | solution.py:277
  11.4 18.0 %collective-permute-start.16 = (bf16[144,896]{1,0:T(8,128)(2,1)S(1)}, bf16[144,896]{1,0:T(8,128)(2,1)S(1)}, u32[]{:S(2)}, u32[]{:S(2)}) collective-permute-start(bf16[144,896]{1,0:T(8,128)(2,1)S(1)} %get-tuple-element.37), channel_id=1, source_target_pairs={{0,2},{2,0},{4,6},{6,4},{1,3},{3,1},{5,7},{7,5},{8,10},{10,8},{12,... | collective-permute-start | bytes 774152 | tf_op jit(solution)/shard_map/ppermute | solution.py:277
  18.0 14.8 %collective-permute-start.29 = (bf16[144,896]{1,0:T(8,128)(2,1)S(1)}, bf16[144,896]{1,0:T(8,128)(2,1)S(1)}, u32[]{:S(2)}, u32[]{:S(2)}) collective-permute-start(bf16[144,896]{1,0:T(8,128)(2,1)S(1)} %get-tuple-element.36.refs_4_.refs_36_), channel_id=1, source_target_pairs={{0,16},{8,24},{16,0},{24,8},{1,17},{9,25},{17,1},{25,9},{2,18},{10... | collective-permute-start | bytes 774152 | tf_op jit(solution)/shard_map/ppermute | solution.py:277
  27.4 6.3 %collective-permute-start.21 = (bf16[144,896]{1,0:T(8,128)(2,1)S(1)}, bf16[144,896]{1,0:T(8,128)(2,1)S(1)}, u32[]{:S(2)}, u32[]{:S(2)}) collective-permute-start(bf16[144,896]{1,0:T(8,128)(2,1)S(1)} %get-tuple-element.36.refs_4_.refs_36_), channel_id=1, source_target_pairs={{0,8},{8,0},{16,24},{24,16},{1,9},{9,1},{17,25},{25,17},{2,10},{10... | collective-permute-start | bytes 774152 | tf_op jit(solution)/shard_map/ppermute | solution.py:277
  28.9 4.8 %collective-permute-start.17 = (bf16[144,896]{1,0:T(8,128)(2,1)S(1)}, bf16[144,896]{1,0:T(8,128)(2,1)S(1)}, u32[]{:S(2)}, u32[]{:S(2)}) collective-permute-start(bf16[144,896]{1,0:T(8,128)(2,1)S(1)} %get-tuple-element.36.refs_4_.refs_36_), channel_id=1, source_target_pairs={{0,1},{1,0},{2,3},{3,2},{4,5},{5,4},{6,7},{7,6},{8,9},{9,8},{10,11... | collective-permute-start | bytes 774152 | tf_op jit(solution)/shard_map/ppermute | solution.py:277
  28.9 6.4 %collective-permute-start.4 = (bf16[144,896]{1,0:T(8,128)(2,1)S(1)}, bf16[144,896]{1,0:T(8,128)(2,1)S(1)}, u32[]{:S(2)}, u32[]{:S(2)}) collective-permute-start(bf16[144,896]{1,0:T(8,128)(2,1)S(1)} %collective-permute-done.refs_1_), channel_id=1, source_target_pairs={{0,1},{1,0},{2,3},{3,2},{4,5},{5,4},{6,7},{7,6},{8,9},{9,8},{10,11... | collective-permute-start | bytes 774152 | tf_op jit(solution)/shard_map/ppermute | solution.py:277
  29.4 10.1 %collective-permute-start.9 = (bf16[144,896]{1,0:T(8,128)(2,1)S(1)}, bf16[144,896]{1,0:T(8,128)(2,1)S(1)}, u32[]{:S(2)}, u32[]{:S(2)}) collective-permute-start(bf16[144,896]{1,0:T(8,128)(2,1)S(1)} %get-tuple-element.31), channel_id=1, source_target_pairs={{0,6},{2,4},{4,2},{6,0},{1,7},{3,5},{5,3},{7,1},{8,14},{10,12},{12... | collective-permute-start | bytes 774152 | tf_op jit(solution)/shard_map/ppermute | solution.py:277
  32.8 6.7 %collective-permute-start.5 = (bf16[144,896]{1,0:T(8,128)(2,1)S(1)}, bf16[144,896]{1,0:T(8,128)(2,1)S(1)}, u32[]{:S(2)}, u32[]{:S(2)}) collective-permute-start(bf16[144,896]{1,0:T(8,128)(2,1)S(1)} %collective-permute-done.1.refs_2_), channel_id=1, source_target_pairs={{0,1},{1,0},{2,3},{3,2},{4,5},{5,4},{6,7},{7,6},{8,9},{9,8},{10,11... | collective-permute-start | bytes 774152 | tf_op jit(solution)/shard_map/ppermute | solution.py:277
  33.7 6.4 %collective-permute-start.6 = (bf16[144,896]{1,0:T(8,128)(2,1)S(1)}, bf16[144,896]{1,0:T(8,128)(2,1)S(1)}, u32[]{:S(2)}, u32[]{:S(2)}) collective-permute-start(bf16[144,896]{1,0:T(8,128)(2,1)S(1)} %collective-permute-done.2.refs_3_), channel_id=1, source_target_pairs={{0,1},{1,0},{2,3},{3,2},{4,5},{5,4},{6,7},{7,6},{8,9},{9,8},{10,11... | collective-permute-start | bytes 774152 | tf_op jit(solution)/shard_map/ppermute | solution.py:277
  33.7 8.6 %collective-permute-start.30 = (bf16[144,896]{1,0:T(8,128)(2,1)S(1)}, bf16[144,896]{1,0:T(8,128)(2,1)S(1)}, u32[]{:S(2)}, u32[]{:S(2)}) collective-permute-start(bf16[144,896]{1,0:T(8,128)(2,1)S(1)} %collective-permute-done.16.refs_5_.refs_37_), channel_id=1, source_target_pairs={{0,16},{8,24},{16,0},{24,8},{1,17},{9,25},{17,1},{25,9},{2,18},{10... | collective-permute-start | bytes 774152 | tf_op jit(solution)/shard_map/ppermute | solution.py:277
  35.2 9.1 %collective-permute-start.22 = (bf16[144,896]{1,0:T(8,128)(2,1)S(1)}, bf16[144,896]{1,0:T(8,128)(2,1)S(1)}, u32[]{:S(2)}, u32[]{:S(2)}) collective-permute-start(bf16[144,896]{1,0:T(8,128)(2,1)S(1)} %collective-permute-done.16.refs_5_.refs_37_), channel_id=1, source_target_pairs={{0,8},{8,0},{16,24},{24,16},{1,9},{9,1},{17,25},{25,17},{2,10},{10... | collective-permute-start | bytes 774152 | tf_op jit(solution)/shard_map/ppermute | solution.py:277
  39.5 8.9 %collective-permute-start.18 = (bf16[144,896]{1,0:T(8,128)(2,1)S(1)}, bf16[144,896]{1,0:T(8,128)(2,1)S(1)}, u32[]{:S(2)}, u32[]{:S(2)}) collective-permute-start(bf16[144,896]{1,0:T(8,128)(2,1)S(1)} %collective-permute-done.16.refs_5_.refs_37_), channel_id=1, source_target_pairs={{0,1},{1,0},{2,3},{3,2},{4,5},{5,4},{6,7},{7,6},{8,9},{9,8},{10,11... | collective-permute-start | bytes 774152 | tf_op jit(solution)/shard_map/ppermute | solution.py:277
  39.5 22.5 %copy-start = (bf16[1,512,3584]{2,1,0:T(8,128)(2,1)S(1)}, bf16[1,512,3584]{2,1,0:T(8,128)(2,1)}, u32[]{:S(2)}) copy-start(bf16[1,512,3584]{2,1,0:T(8,128)(2,1)} %w_ref.1) | copy-start | bytes 11010052
  39.5 16.5 %collective-permute-start.37 = (bf16[144,896]{1,0:T(8,128)(2,1)S(1)}, bf16[144,896]{1,0:T(8,128)(2,1)S(1)}, u32[]{:S(2)}, u32[]{:S(2)}) collective-permute-start(bf16[144,896]{1,0:T(8,128)(2,1)S(1)} %collective-permute-done.29.refs_20_.refs_52_), channel_id=1, source_target_pairs={{0,8},{8,0},{16,24},{24,16},{1,9},{9,1},{17,25},{25,17},{2,10},{10... | collective-permute-start | bytes 774152 | tf_op jit(solution)/shard_map/ppermute | solution.py:277
  40.1 16.7 %collective-permute-start.33 = (bf16[144,896]{1,0:T(8,128)(2,1)S(1)}, bf16[144,896]{1,0:T(8,128)(2,1)S(1)}, u32[]{:S(2)}, u32[]{:S(2)}) collective-permute-start(bf16[144,896]{1,0:T(8,128)(2,1)S(1)} %collective-permute-done.29.refs_20_.refs_52_), channel_id=1, source_target_pairs={{0,1},{1,0},{2,3},{3,2},{4,5},{5,4},{6,7},{7,6},{8,9},{9,8},{10,11... | collective-permute-start | bytes 774152 | tf_op jit(solution)/shard_map/ppermute | solution.py:277
  42.3 14.5 %collective-permute-start.25 = (bf16[144,896]{1,0:T(8,128)(2,1)S(1)}, bf16[144,896]{1,0:T(8,128)(2,1)S(1)}, u32[]{:S(2)}, u32[]{:S(2)}) collective-permute-start(bf16[144,896]{1,0:T(8,128)(2,1)S(1)} %collective-permute-done.21.refs_12_.refs_44_), channel_id=1, source_target_pairs={{0,1},{1,0},{2,3},{3,2},{4,5},{5,4},{6,7},{7,6},{8,9},{9,8},{10,11... | collective-permute-start | bytes 774152 | tf_op jit(solution)/shard_map/ppermute | solution.py:277
  44.3 16.2 %collective-permute-start.10 = (bf16[144,896]{1,0:T(8,128)(2,1)S(1)}, bf16[144,896]{1,0:T(8,128)(2,1)S(1)}, u32[]{:S(2)}, u32[]{:S(2)}) collective-permute-start(bf16[144,896]{1,0:T(8,128)(2,1)S(1)} %get-tuple-element.32), channel_id=1, source_target_pairs={{0,4},{2,6},{4,0},{6,2},{1,5},{3,7},{5,1},{7,3},{8,12},{10,14},{12... | collective-permute-start | bytes 774152 | tf_op jit(solution)/shard_map/ppermute | solution.py:277
  48.4 17.7 %collective-permute-start.32 = (bf16[144,896]{1,0:T(8,128)(2,1)S(1)}, bf16[144,896]{1,0:T(8,128)(2,1)S(1)}, u32[]{:S(2)}, u32[]{:S(2)}) collective-permute-start(bf16[144,896]{1,0:T(8,128)(2,1)S(1)} %collective-permute-done.9.refs_7_.refs_39_), channel_id=1, source_target_pairs={{0,16},{8,24},{16,0},{24,8},{1,17},{9,25},{17,1},{25,9},{2,18},{10... | collective-permute-start | bytes 774152 | tf_op jit(solution)/shard_map/ppermute | solution.py:277
  56.0 10.2 %collective-permute-start.24 = (bf16[144,896]{1,0:T(8,128)(2,1)S(1)}, bf16[144,896]{1,0:T(8,128)(2,1)S(1)}, u32[]{:S(2)}, u32[]{:S(2)}) collective-permute-start(bf16[144,896]{1,0:T(8,128)(2,1)S(1)} %collective-permute-done.9.refs_7_.refs_39_), channel_id=1, source_target_pairs={{0,8},{8,0},{16,24},{24,16},{1,9},{9,1},{17,25},{25,17},{2,10},{10... | collective-permute-start | bytes 774152 | tf_op jit(solution)/shard_map/ppermute | solution.py:277
  56.8 10.0 %collective-permute-start.20 = (bf16[144,896]{1,0:T(8,128)(2,1)S(1)}, bf16[144,896]{1,0:T(8,128)(2,1)S(1)}, u32[]{:S(2)}, u32[]{:S(2)}) collective-permute-start(bf16[144,896]{1,0:T(8,128)(2,1)S(1)} %collective-permute-done.9.refs_7_.refs_39_), channel_id=1, source_target_pairs={{0,1},{1,0},{2,3},{3,2},{4,5},{5,4},{6,7},{7,6},{8,9},{9,8},{10,11... | collective-permute-start | bytes 774152 | tf_op jit(solution)/shard_map/ppermute | solution.py:277
  56.8 10.6 %collective-permute-start.34 = (bf16[144,896]{1,0:T(8,128)(2,1)S(1)}, bf16[144,896]{1,0:T(8,128)(2,1)S(1)}, u32[]{:S(2)}, u32[]{:S(2)}) collective-permute-start(bf16[144,896]{1,0:T(8,128)(2,1)S(1)} %collective-permute-done.30.refs_21_.refs_53_), channel_id=1, source_target_pairs={{0,1},{1,0},{2,3},{3,2},{4,5},{5,4},{6,7},{7,6},{8,9},{9,8},{10,11... | collective-permute-start | bytes 774152 | tf_op jit(solution)/shard_map/ppermute | solution.py:277
  60.5 8.4 %collective-permute-start.38 = (bf16[144,896]{1,0:T(8,128)(2,1)S(1)}, bf16[144,896]{1,0:T(8,128)(2,1)S(1)}, u32[]{:S(2)}, u32[]{:S(2)}) collective-permute-start(bf16[144,896]{1,0:T(8,128)(2,1)S(1)} %collective-permute-done.22.refs_13_.refs_45_), channel_id=1, source_target_pairs={{0,16},{8,24},{16,0},{24,8},{1,17},{9,25},{17,1},{25,9},{2,18},{10... | collective-permute-start | bytes 774152 | tf_op jit(solution)/shard_map/ppermute | solution.py:277
  66.2 31.5 %collective-permute-start.7 = (bf16[4,144,896]{2,1,0:T(8,128)(2,1)S(1)}, bf16[4,144,896]{2,1,0:T(8,128)(2,1)S(1)}, u32[]{:S(2)}, u32[]{:S(2)}) collective-permute-start(bf16[4,144,896]{2,1,0:T(8,128)(2,1)S(1)} %get-tuple-element.25), channel_id=1, source_target_pairs={{0,1},{1,0},{2,3},{3,2},{4,5},{5,4},{6,7},{7,6},{8,9},{9,8},{10,11... | collective-permute-start | bytes 3096584 | tf_op jit(solution)/shard_map/ppermute | solution.py:277
  66.3 3.0 %collective-permute-start.26 = (bf16[144,896]{1,0:T(8,128)(2,1)S(1)}, bf16[144,896]{1,0:T(8,128)(2,1)S(1)}, u32[]{:S(2)}, u32[]{:S(2)}) collective-permute-start(bf16[144,896]{1,0:T(8,128)(2,1)S(1)} %collective-permute-done.22.refs_13_.refs_45_), channel_id=1, source_target_pairs={{0,1},{1,0},{2,3},{3,2},{4,5},{5,4},{6,7},{7,6},{8,9},{9,8},{10,11... | collective-permute-start | bytes 774152 | tf_op jit(solution)/shard_map/ppermute | solution.py:277
  66.8 10.8 %collective-permute-start.15 = (bf16[288,512]{1,0:T(8,128)(2,1)S(1)}, bf16[288,512]{1,0:T(8,128)(2,1)S(1)}, u32[]{:S(2)}, u32[]{:S(2)}) collective-permute-start(bf16[288,512]{1,0:T(8,128)(2,1)S(1)} %shard_map.87.hidden_ref.refs_0_), channel_id=1, source_target_pairs={{0,24},{8,16},{16,8},{24,0},{1,25},{9,17},{17,9},{25,1},{2,26},{10... | collective-permute-start | bytes 884744 | tf_op jit(solution)/shard_map/ppermute | solution.py:277
  67.4 15.7 %collective-permute-start.14 = (bf16[288,512]{1,0:T(8,128)(2,1)S(1)}, bf16[288,512]{1,0:T(8,128)(2,1)S(1)}, u32[]{:S(2)}, u32[]{:S(2)}) collective-permute-start(bf16[288,512]{1,0:T(8,128)(2,1)S(1)} %shard_map.87.hidden_ref.refs_0_), channel_id=1, source_target_pairs={{0,16},{8,24},{16,0},{24,8},{1,17},{9,25},{17,1},{25,9},{2,18},{10... | collective-permute-start | bytes 884744 | tf_op jit(solution)/shard_map/ppermute | solution.py:277
  68.9 1.5 %collective-permute-start.41 = (bf16[144,896]{1,0:T(8,128)(2,1)S(1)}, bf16[144,896]{1,0:T(8,128)(2,1)S(1)}, u32[]{:S(2)}, u32[]{:S(2)}) collective-permute-start(bf16[144,896]{1,0:T(8,128)(2,1)S(1)} %collective-permute-done.37.refs_28_.refs_60_), channel_id=1, source_target_pairs={{0,1},{1,0},{2,3},{3,2},{4,5},{5,4},{6,7},{7,6},{8,9},{9,8},{10,11... | collective-permute-start | bytes 774152 | tf_op jit(solution)/shard_map/ppermute | solution.py:277
  69.3 13.9 %collective-permute-start.13 = (bf16[288,512]{1,0:T(8,128)(2,1)S(1)}, bf16[288,512]{1,0:T(8,128)(2,1)S(1)}, u32[]{:S(2)}, u32[]{:S(2)}) collective-permute-start(bf16[288,512]{1,0:T(8,128)(2,1)S(1)} %shard_map.87.hidden_ref.refs_0_), channel_id=1, source_target_pairs={{0,8},{8,0},{16,24},{24,16},{1,9},{9,1},{17,25},{25,17},{2,10},{10... | collective-permute-start | bytes 884744 | tf_op jit(solution)/shard_map/ppermute | solution.py:277
  70.4 17.5 %collective-permute-start.31 = (bf16[144,896]{1,0:T(8,128)(2,1)S(1)}, bf16[144,896]{1,0:T(8,128)(2,1)S(1)}, u32[]{:S(2)}, u32[]{:S(2)}) collective-permute-start(bf16[144,896]{1,0:T(8,128)(2,1)S(1)} %collective-permute-done.10.refs_6_.refs_38_), channel_id=1, source_target_pairs={{0,16},{8,24},{16,0},{24,8},{1,17},{9,25},{17,1},{25,9},{2,18},{10... | collective-permute-start | bytes 774152 | tf_op jit(solution)/shard_map/ppermute | solution.py:277
  77.6 11.5 %collective-permute-start.23 = (bf16[144,896]{1,0:T(8,128)(2,1)S(1)}, bf16[144,896]{1,0:T(8,128)(2,1)S(1)}, u32[]{:S(2)}, u32[]{:S(2)}) collective-permute-start(bf16[144,896]{1,0:T(8,128)(2,1)S(1)} %collective-permute-done.10.refs_6_.refs_38_), channel_id=1, source_target_pairs={{0,8},{8,0},{16,24},{24,16},{1,9},{9,1},{17,25},{25,17},{2,10},{10... | collective-permute-start | bytes 774152 | tf_op jit(solution)/shard_map/ppermute | solution.py:277
  83.1 6.0 %collective-permute-start.19 = (bf16[144,896]{1,0:T(8,128)(2,1)S(1)}, bf16[144,896]{1,0:T(8,128)(2,1)S(1)}, u32[]{:S(2)}, u32[]{:S(2)}) collective-permute-start(bf16[144,896]{1,0:T(8,128)(2,1)S(1)} %collective-permute-done.10.refs_6_.refs_38_), channel_id=1, source_target_pairs={{0,1},{1,0},{2,3},{3,2},{4,5},{5,4},{6,7},{7,6},{8,9},{9,8},{10,11... | collective-permute-start | bytes 774152 | tf_op jit(solution)/shard_map/ppermute | solution.py:277
  83.1 6.7 %collective-permute-start.36 = (bf16[144,896]{1,0:T(8,128)(2,1)S(1)}, bf16[144,896]{1,0:T(8,128)(2,1)S(1)}, u32[]{:S(2)}, u32[]{:S(2)}) collective-permute-start(bf16[144,896]{1,0:T(8,128)(2,1)S(1)} %collective-permute-done.32.refs_23_.refs_55_), channel_id=1, source_target_pairs={{0,1},{1,0},{2,3},{3,2},{4,5},{5,4},{6,7},{7,6},{8,9},{9,8},{10,11... | collective-permute-start | bytes 774152 | tf_op jit(solution)/shard_map/ppermute | solution.py:277
  88.0 7.6 %collective-permute-start.40 = (bf16[144,896]{1,0:T(8,128)(2,1)S(1)}, bf16[144,896]{1,0:T(8,128)(2,1)S(1)}, u32[]{:S(2)}, u32[]{:S(2)}) collective-permute-start(bf16[144,896]{1,0:T(8,128)(2,1)S(1)} %collective-permute-done.24.refs_15_.refs_47_), channel_id=1, source_target_pairs={{0,16},{8,24},{16,0},{24,8},{1,17},{9,25},{17,1},{25,9},{2,18},{10... | collective-permute-start | bytes 774152 | tf_op jit(solution)/shard_map/ppermute | solution.py:277
  89.0 6.5 %collective-permute-start.28 = (bf16[144,896]{1,0:T(8,128)(2,1)S(1)}, bf16[144,896]{1,0:T(8,128)(2,1)S(1)}, u32[]{:S(2)}, u32[]{:S(2)}) collective-permute-start(bf16[144,896]{1,0:T(8,128)(2,1)S(1)} %collective-permute-done.24.refs_15_.refs_47_), channel_id=1, source_target_pairs={{0,1},{1,0},{2,3},{3,2},{4,5},{5,4},{6,7},{7,6},{8,9},{9,8},{10,11... | collective-permute-start | bytes 774152 | tf_op jit(solution)/shard_map/ppermute | solution.py:277
  89.1 8.6 %collective-permute-start.39 = (bf16[144,896]{1,0:T(8,128)(2,1)S(1)}, bf16[144,896]{1,0:T(8,128)(2,1)S(1)}, u32[]{:S(2)}, u32[]{:S(2)}) collective-permute-start(bf16[144,896]{1,0:T(8,128)(2,1)S(1)} %collective-permute-done.31.refs_22_.refs_54_), channel_id=1, source_target_pairs={{0,8},{8,0},{16,24},{24,16},{1,9},{9,1},{17,25},{25,17},{2,10},{10... | collective-permute-start | bytes 774152 | tf_op jit(solution)/shard_map/ppermute | solution.py:277
  89.8 8.7 %collective-permute-start.42 = (bf16[144,896]{1,0:T(8,128)(2,1)S(1)}, bf16[144,896]{1,0:T(8,128)(2,1)S(1)}, u32[]{:S(2)}, u32[]{:S(2)}) collective-permute-start(bf16[144,896]{1,0:T(8,128)(2,1)S(1)} %collective-permute-done.38.refs_29_.refs_61_), channel_id=1, source_target_pairs={{0,1},{1,0},{2,3},{3,2},{4,5},{5,4},{6,7},{7,6},{8,9},{9,8},{10,11... | collective-permute-start | bytes 774152 | tf_op jit(solution)/shard_map/ppermute | solution.py:277
  95.5 3.5 %collective-permute-start.35 = (bf16[144,896]{1,0:T(8,128)(2,1)S(1)}, bf16[144,896]{1,0:T(8,128)(2,1)S(1)}, u32[]{:S(2)}, u32[]{:S(2)}) collective-permute-start(bf16[144,896]{1,0:T(8,128)(2,1)S(1)} %collective-permute-done.31.refs_22_.refs_54_), channel_id=1, source_target_pairs={{0,1},{1,0},{2,3},{3,2},{4,5},{5,4},{6,7},{7,6},{8,9},{9,8},{10,11... | collective-permute-start | bytes 774152 | tf_op jit(solution)/shard_map/ppermute | solution.py:277
  95.5 3.5 %collective-permute-start.27 = (bf16[144,896]{1,0:T(8,128)(2,1)S(1)}, bf16[144,896]{1,0:T(8,128)(2,1)S(1)}, u32[]{:S(2)}, u32[]{:S(2)}) collective-permute-start(bf16[144,896]{1,0:T(8,128)(2,1)S(1)} %collective-permute-done.23.refs_14_.refs_46_), channel_id=1, source_target_pairs={{0,1},{1,0},{2,3},{3,2},{4,5},{5,4},{6,7},{7,6},{8,9},{9,8},{10,11... | collective-permute-start | bytes 774152 | tf_op jit(solution)/shard_map/ppermute | solution.py:277
  97.7 5.2 %collective-permute-start.44 = (bf16[144,896]{1,0:T(8,128)(2,1)S(1)}, bf16[144,896]{1,0:T(8,128)(2,1)S(1)}, u32[]{:S(2)}, u32[]{:S(2)}) collective-permute-start(bf16[144,896]{1,0:T(8,128)(2,1)S(1)} %collective-permute-done.40.refs_31_.refs_63_), channel_id=1, source_target_pairs={{0,1},{1,0},{2,3},{3,2},{4,5},{5,4},{6,7},{7,6},{8,9},{9,8},{10,11... | collective-permute-start | bytes 774152 | tf_op jit(solution)/shard_map/ppermute | solution.py:277
  97.7 5.2 %collective-permute-start.43 = (bf16[144,896]{1,0:T(8,128)(2,1)S(1)}, bf16[144,896]{1,0:T(8,128)(2,1)S(1)}, u32[]{:S(2)}, u32[]{:S(2)}) collective-permute-start(bf16[144,896]{1,0:T(8,128)(2,1)S(1)} %collective-permute-done.39.refs_30_.refs_62_), channel_id=1, source_target_pairs={{0,1},{1,0},{2,3},{3,2},{4,5},{5,4},{6,7},{7,6},{8,9},{9,8},{10,11... | collective-permute-start | bytes 774152 | tf_op jit(solution)/shard_map/ppermute | solution.py:277
  98.5 12.4 %collective-permute-start.12 = (bf16[144,896]{1,0:T(8,128)(2,1)S(1)}, bf16[144,896]{1,0:T(8,128)(2,1)S(1)}, u32[]{:S(2)}, u32[]{:S(2)}) collective-permute-start(bf16[144,896]{1,0:T(8,128)(2,1)S(1)} %get-tuple-element.35), channel_id=1, source_target_pairs={{0,6},{2,4},{4,2},{6,0},{1,7},{3,5},{5,3},{7,1},{8,14},{10,12},{12... | collective-permute-start | bytes 774152 | tf_op jit(solution)/shard_map/ppermute | solution.py:277
  99.0 22.0 %collective-permute-start.11 = (bf16[144,896]{1,0:T(8,128)(2,1)S(1)}, bf16[144,896]{1,0:T(8,128)(2,1)S(1)}, u32[]{:S(2)}, u32[]{:S(2)}) collective-permute-start(bf16[144,896]{1,0:T(8,128)(2,1)S(1)} %get-tuple-element.33), channel_id=1, source_target_pairs={{0,4},{2,6},{4,0},{6,2},{1,5},{3,7},{5,1},{7,3},{8,12},{10,14},{12... | collective-permute-start | bytes 774152 | tf_op jit(solution)/shard_map/ppermute | solution.py:277
  99.0 22.0 %copy-start.4 = (s32[128,1]{0,1:T(1,128)S(1)}, s32[128,1]{0,1:T(1,128)}, u32[]{:S(2)}) copy-start(s32[128,1]{0,1:T(1,128)} %param.9) | copy-start | bytes 1540
  99.1 22.0 %copy-start.6 = (f32[128,1]{0,1:T(1,128)S(1)}, f32[128,1]{0,1:T(1,128)}, u32[]{:S(2)}) copy-start(f32[128,1]{0,1:T(1,128)} %param.10) | copy-start | bytes 1540
  99.1 22.0 %collective-permute-start.8 = (bf16[144,896]{1,0:T(8,128)(2,1)S(1)}, bf16[144,896]{1,0:T(8,128)(2,1)S(1)}, u32[]{:S(2)}, u32[]{:S(2)}) collective-permute-start(bf16[144,896]{1,0:T(8,128)(2,1)S(1)} %get-tuple-element.27), channel_id=1, source_target_pairs={{0,2},{2,0},{4,6},{6,4},{1,3},{3,1},{5,7},{7,5},{8,10},{10,8},{12,... | collective-permute-start | bytes 774152 | tf_op jit(solution)/shard_map/ppermute | solution.py:277
  (4 other events, 3.7 us)
